TPU v7x, 256 devices: a whole 4x4x8 slice. The times are simulated.
256 devices in a mesh: ctx: 16 (over x, y_hi, core), tp: 16 (over y_lo, z).
Axes of the slice: x: 4, y: 4 (y_hi: 2, y_lo: 2; y = y_hi * 2 + y_lo), z: 8, core: 2. Of those that a mesh axis runs over, the one named last changes fastest.
Arguments:
- gate_proj: bfloat16 [4096, 4096], P('ctx', 'tp'), may hold values from -6 to 6
- key_proj: bfloat16 [4096, 4096], P('ctx', 'tp'), may hold values from -6 to 6
- value_proj: bfloat16 [4096, 4096], P('ctx', 'tp'), may hold values from -6 to 6
- stream: bfloat16 [4096, 4096], P('ctx', 'tp'), may hold values from -60 to 60
- decay_rate: float32 [16, 4096], P(None, 'tp'), may hold values from 0 to 1
- residue: float32 [16, 4096], P(None, 'tp'), may hold values from -2 to 2
- norm_gain: float32 [4096], P('tp'), may hold values from 0.1 to 1.9
- query_att: bfloat16 [4096, 4096], P('ctx', 'tp'), may hold values from -5 to 5
- key_att: bfloat16 [4096, 4096], P('ctx', 'tp'), may hold values from -5 to 5
- out_grad: bfloat16 [4096, 4096], P('ctx', 'tp'), may hold values from -6 to 6
Outputs:
- attended: bfloat16 [4096, 4096], P('ctx', 'tp')
- gate_grad: bfloat16 [4096, 4096], P('ctx', 'tp')
- keyproj_grad: bfloat16 [4096, 4096], P('ctx', 'tp')
- value_grad: bfloat16 [4096, 4096], P('ctx', 'tp')
- stream_grad: bfloat16 [4096, 4096], P('ctx', 'tp')
- gain_grad: float32 [4096], P('tp')
- query_grad: bfloat16 [4096, 4096], P('ctx', 'tp')
- keyatt_grad: bfloat16 [4096, 4096], P('ctx', 'tp')
All inputs are finite; a program needn't handle non-finite values.
Results may differ from a plain program's by a relative error of at most 0.03.
Values may be sent and summed in bfloat16 or wider, within the bound.
A program may use at most 64 MiB of HBM per device.

v0:
```python
import jax
import jax.numpy as jnp
from jax import lax
from jax.sharding import PartitionSpec as P

HD = 128


NEG_FILL = -1e30
NORM_EPS = 1e-06
HIGHEST = lax.Precision.HIGHEST


def entering_2(shard, axis, combine, identity):
    size, place = (lax.axis_size(axis), lax.axis_index(axis))
    everything = jax.tree.map(
        lambda part, kind: lax.all_gather(part.astype(kind), axis),
        shard,
        (jnp.bfloat16, jnp.bfloat16),
    )
    start = jax.tree.map(
        lambda part, zero: jnp.broadcast_to(jnp.asarray(zero, part.dtype), part.shape),
        shard,
        identity,
    )

    def hop(k, before):
        reached = k < place
        new = combine(
            before, jax.tree.map(lambda part, own: part[k].astype(own.dtype), everything, shard)
        )
        return jax.tree.map(lambda a, b: jnp.where(reached, a, b), new, before)

    return lax.fori_loop(0, size, hop, start)


def entering_3(shard, axis, join, neutral):
    count = lax.axis_size(axis)
    place = lax.axis_index(axis)
    ahead = count - 1 - place
    gathered = jax.tree.map(
        lambda a, kind: lax.all_gather(a.astype(kind), axis),
        shard,
        jax.tree.map(lambda a: jnp.bfloat16 if a.dtype == jnp.float32 else a.dtype, shard),
    )
    state = jax.tree.map(lambda a, e: jnp.zeros_like(a) + jnp.asarray(e, a.dtype), shard, neutral)

    def one(hop, state):
        source = count - 1 - hop
        return join(
            state,
            jax.tree.map(
                lambda a, own: lax.dynamic_index_in_dim(a, source, 0, False).astype(own.dtype),
                gathered,
                shard,
            ),
        )

    return lax.fori_loop(0, ahead, one, state)


def block_span():
    return 512


def unchanged(running):
    return running


def chain_merge(earlier, later):
    return (earlier[0] * later[0], later[0] * earlier[1] + later[1])


def modal_local(signal, decay_rate, residue):
    tok_rows, chan_loc = signal.shape
    width = 64
    block_count = tok_rows // width
    offsets = jnp.arange(width, dtype=jnp.float32)
    powers = jnp.exp(-decay_rate[None] * offsets[:, None, None])
    kernel = jnp.sum(residue[None] * powers, axis=1)
    lag_index = jnp.arange(width)[:, None] - jnp.arange(width)[None, :]
    toeplitz = jnp.where((lag_index >= 0)[:, :, None], kernel[jnp.maximum(lag_index, 0)], 0.0)
    blocks = signal.reshape(block_count, width, chan_loc)
    inner = jnp.einsum("abc,nbc->nac", toeplitz, blocks, precision=HIGHEST)
    tails = jnp.exp(-decay_rate[None] * (width - 1.0 - offsets)[:, None, None])
    block_ends = jnp.einsum("bmc,nbc->nmc", tails, blocks, precision=HIGHEST)
    block_decay = jnp.exp(-decay_rate * width)
    running = jnp.zeros_like(decay_rate)
    entries = []
    for number in range(block_count):
        entries.append(running)
        running = block_decay * running + block_ends[number]
    return (inner, jnp.stack(entries), running, offsets, width)


def modal_finish(inner, entries, incoming, decay_rate, residue, offsets, width):
    block_count = entries.shape[0]
    shifts = jnp.exp(
        -decay_rate[None] * (width * jnp.arange(block_count, dtype=jnp.float32))[:, None, None]
    )
    entry_states = entries + shifts * incoming[None]
    leading = residue[None] * jnp.exp(-decay_rate[None] * (offsets + 1.0)[:, None, None])
    outer = jnp.einsum("amc,nmc->nac", leading, entry_states, precision=HIGHEST)
    return (inner + outer).reshape(block_count * width, -1)


def attend_block(running, query_heads, query_pos, key_heads, value_heads, key_pos, scale):
    top, total, accum = running
    scores = (
        jnp.einsum("shd,khd->hsk", query_heads, key_heads, preferred_element_type=jnp.float32)
        * scale
    )
    allowed = query_pos[:, None] >= key_pos[None, :]
    scores = jnp.where(allowed[None], scores, NEG_FILL)
    new_top = jnp.maximum(top, jnp.max(scores, axis=2))
    exps = jnp.exp(scores - new_top[:, :, None])
    factor = jnp.exp(top - new_top)
    total = total * factor + jnp.sum(exps, axis=2)
    update = jnp.einsum(
        "hsk,khd->shd", exps.astype(jnp.bfloat16), value_heads, preferred_element_type=jnp.float32
    )
    accum = accum * jnp.transpose(factor)[:, :, None] + update
    return (new_top, total, accum)


def pair_grads(
    query_heads, grad_heads, log_total, delta, query_pos, key_heads, value_heads, key_pos, scale
):
    scores = (
        jnp.einsum("qhd,khd->hqk", query_heads, key_heads, preferred_element_type=jnp.float32)
        * scale
    )
    allowed = query_pos[:, None] >= key_pos[None, :]
    probs = jnp.where(allowed[None], jnp.exp(scores - log_total[:, :, None]), 0.0)
    value_part = jnp.einsum(
        "hqk,qhd->khd", probs.astype(jnp.bfloat16), grad_heads, preferred_element_type=jnp.float32
    )
    prob_grad = jnp.einsum(
        "qhd,khd->hqk", grad_heads, value_heads, preferred_element_type=jnp.float32
    )
    score_grad = (probs * (prob_grad - delta[:, :, None])).astype(jnp.bfloat16)
    query_part = (
        jnp.einsum("hqk,khd->qhd", score_grad, key_heads, preferred_element_type=jnp.float32)
        * scale
    )
    key_part = (
        jnp.einsum("hqk,qhd->khd", score_grad, query_heads, preferred_element_type=jnp.float32)
        * scale
    )
    return (query_part, key_part, value_part)


def on_device(
    gate_proj,
    key_proj,
    value_proj,
    stream,
    decay_rate,
    residue,
    norm_gain,
    query_att,
    key_att,
    out_grad,
):
    tok_rows, chan_loc = stream.shape
    head_loc = chan_loc // HD
    chan_all = chan_loc * lax.axis_size("tp")
    my_index = lax.axis_index("ctx")
    scale = HD ** (-0.5)
    mixed = key_proj.astype(jnp.float32) * value_proj.astype(jnp.float32)
    inner, entries, end_state, offsets, width = modal_local(mixed, decay_rate, residue)
    local_decay = jnp.exp(-decay_rate * tok_rows)
    identity = (jnp.ones_like(local_decay), jnp.zeros_like(end_state))
    entering = entering_2((local_decay, end_state), "ctx", chain_merge, identity)[1]
    conv = modal_finish(inner, entries, entering, decay_rate, residue, offsets, width)
    gate = gate_proj.astype(jnp.float32)
    summed = stream.astype(jnp.float32) + gate * conv
    squares = lax.psum(jnp.sum(summed * summed, axis=1), "tp")
    inverse = lax.rsqrt(squares / chan_all + NORM_EPS)[:, None]
    normed = summed * inverse
    values = (normed * norm_gain[None, :]).astype(jnp.bfloat16)
    query_heads = query_att.reshape(tok_rows, head_loc, HD)
    key_heads = key_att.reshape(tok_rows, head_loc, HD)
    value_heads = values.reshape(tok_rows, head_loc, HD)
    grad_heads = out_grad.reshape(tok_rows, head_loc, HD)
    query_pos = my_index * tok_rows + jnp.arange(tok_rows, dtype=jnp.int32)
    start_state = (
        jnp.full((head_loc, tok_rows), NEG_FILL, jnp.float32),
        jnp.zeros((head_loc, tok_rows), jnp.float32),
        jnp.zeros((tok_rows, head_loc, HD), jnp.float32),
    )
    running = start_state
    keys_piece = lax.all_gather(key_att, "ctx", axis=0, tiled=True)
    vals_piece = lax.all_gather(values, "ctx", axis=0, tiled=True)
    count = keys_piece.shape[0]
    span = block_span()
    key_blocks = keys_piece.reshape(count // span, span, head_loc, HD)
    val_blocks = vals_piece.reshape(count // span, span, head_loc, HD)
    block_starts = span * jnp.arange(count // span, dtype=jnp.int32)

    def forward_visit(acc_state, element):
        key_blk, val_blk, first_pos = element
        key_pos = first_pos + jnp.arange(span, dtype=jnp.int32)

        def attend(inner_state):
            return attend_block(
                inner_state, query_heads, query_pos, key_blk, val_blk, key_pos, scale
            )

        return (lax.cond(first_pos <= query_pos[-1], attend, unchanged, acc_state), None)

    running, _ = lax.scan(forward_visit, running, (key_blocks, val_blocks, block_starts))
    top, total, accum = running
    attended = (
        (accum / jnp.transpose(total)[:, :, None]).astype(jnp.bfloat16).reshape(tok_rows, chan_loc)
    )
    log_total = top + jnp.log(total)
    delta = jnp.transpose(
        jnp.sum(
            (out_grad.astype(jnp.float32) * attended.astype(jnp.float32)).reshape(
                tok_rows, head_loc, HD
            ),
            axis=2,
        )
    )
    zero_heads = jnp.zeros((tok_rows, head_loc, HD), jnp.float32)
    running = zero_heads
    keys_piece = lax.all_gather(key_att, "ctx", axis=0, tiled=True)
    vals_piece = lax.all_gather(values, "ctx", axis=0, tiled=True)
    count = keys_piece.shape[0]
    query_span = block_span()
    key_blocks = keys_piece.reshape(count // query_span, query_span, head_loc, HD)
    val_blocks = vals_piece.reshape(count // query_span, query_span, head_loc, HD)
    block_starts = query_span * jnp.arange(count // query_span, dtype=jnp.int32)

    def query_visit(acc_grad, element):
        key_blk, val_blk, first_pos = element
        key_pos = first_pos + jnp.arange(query_span, dtype=jnp.int32)

        def query_work(inner_grad):
            return (
                inner_grad
                + pair_grads(
                    query_heads,
                    grad_heads,
                    log_total,
                    delta,
                    query_pos,
                    key_blk,
                    val_blk,
                    key_pos,
                    scale,
                )[0]
            )

        return (lax.cond(first_pos <= query_pos[-1], query_work, unchanged, acc_grad), None)

    running, _ = lax.scan(query_visit, running, (key_blocks, val_blocks, block_starts))
    query_sum = running
    all_total, all_delta = (
        lax.all_gather(log_total, "ctx", axis=1, tiled=True),
        lax.all_gather(delta, "ctx", axis=1, tiled=True),
    )
    running = (zero_heads, zero_heads)
    queries_piece = lax.all_gather(query_att, "ctx", axis=0, tiled=True)
    grads_piece = lax.all_gather(out_grad, "ctx", axis=0, tiled=True)
    count = queries_piece.shape[0]
    key_span = block_span()
    query_blocks = queries_piece.reshape(count // key_span, key_span, head_loc, HD)
    grad_blocks = grads_piece.reshape(count // key_span, key_span, head_loc, HD)
    block_starts = key_span * jnp.arange(count // key_span, dtype=jnp.int32)

    def key_visit(acc_pair, element):
        query_blk, grad_blk, first_pos = element
        pos_blk = first_pos + jnp.arange(key_span, dtype=jnp.int32)
        total_blk = lax.dynamic_slice_in_dim(all_total, first_pos, key_span, 1)
        delta_blk = lax.dynamic_slice_in_dim(all_delta, first_pos, key_span, 1)

        def key_work(inner_pair):
            parts = pair_grads(
                query_blk,
                grad_blk,
                total_blk,
                delta_blk,
                pos_blk,
                key_heads,
                value_heads,
                query_pos,
                scale,
            )
            return (inner_pair[0] + parts[1], inner_pair[1] + parts[2])

        return (lax.cond(pos_blk[-1] >= query_pos[0], key_work, unchanged, acc_pair), None)

    running, _ = lax.scan(key_visit, running, (query_blocks, grad_blocks, block_starts))
    key_sum, value_sum = running
    key_grad = key_sum.reshape(tok_rows, chan_loc)
    dvalues = value_sum.reshape(tok_rows, chan_loc)
    query_grad = query_sum.reshape(tok_rows, chan_loc).astype(jnp.bfloat16)
    keyatt_grad = key_grad.astype(jnp.bfloat16)
    gain_grad = lax.psum(jnp.sum(dvalues * normed, axis=0), "ctx")
    dnormed = dvalues * norm_gain[None, :]
    row_dot = lax.psum(jnp.sum(dnormed * normed, axis=1), "tp")
    dsummed = inverse * (dnormed - normed * (row_dot / chan_all)[:, None])
    stream_grad = dsummed.astype(jnp.bfloat16)
    gate_grad = (dsummed * conv).astype(jnp.bfloat16)
    flipped = (dsummed * gate)[::-1]
    inner_back, entries_back, end_back, _, _ = modal_local(flipped, decay_rate, residue)
    leaving = entering_3((local_decay, end_back), "ctx", chain_merge, identity)[1]
    dmixed = modal_finish(inner_back, entries_back, leaving, decay_rate, residue, offsets, width)[
        ::-1
    ]
    keyproj_grad = (dmixed * value_proj.astype(jnp.float32)).astype(jnp.bfloat16)
    value_grad = (dmixed * key_proj.astype(jnp.float32)).astype(jnp.bfloat16)
    return (
        attended,
        gate_grad,
        keyproj_grad,
        value_grad,
        stream_grad,
        gain_grad,
        query_grad,
        keyatt_grad,
    )


def solution(mesh):
    return jax.shard_map(
        on_device,
        mesh=mesh,
        in_specs=(
            P("ctx", "tp"),
            P("ctx", "tp"),
            P("ctx", "tp"),
            P("ctx", "tp"),
            P(None, "tp"),
            P(None, "tp"),
            P("tp"),
            P("ctx", "tp"),
            P("ctx", "tp"),
            P("ctx", "tp"),
        ),
        out_specs=(
            P("ctx", "tp"),
            P("ctx", "tp"),
            P("ctx", "tp"),
            P("ctx", "tp"),
            P("ctx", "tp"),
            P("tp"),
            P("ctx", "tp"),
            P("ctx", "tp"),
        ),
        check_vma=False,
    )
```

profile of v0, /device:TPU:1, one launch (start us, length us, event | category | flops | bytes accessed | tf_op | source)
XLA Modules:
  0.0 617.5 jit_solution(10325113551107477892)
XLA Ops:
  9.5 3.5 fusion.80
  13.6 26.0 %all-gather = bf16[256,256]{1,0:T(8,128)(2,1)S(1)} all-gather(bf16[16,256]{1,0:T(8,128)(2,1)S(1)} %exponential_convert_fusion), channel_id=2, replica_groups=mesh['ctx'=16,'tp'=16] {'ctx'}, dimensions={0}, use_global_device_ids=true | all-gather | bytes 139264 | tf_op jit(solution)/shard_map/all_gather | solution.py:17
  39.7 19.8 %all-gather.1 = bf16[256,256]{1,0:T(8,128)(2,1)S(1)} all-gather(bf16[16,256]{1,0:T(8,128)(2,1)S(1)} %copy.158), channel_id=3, replica_groups=mesh['ctx'=16,'tp'=16] {'ctx'}, dimensions={0}, use_global_device_ids=true | all-gather | bytes 139264 | tf_op jit(solution)/shard_map/all_gather | solution.py:17
  63.1 16.1 %gather_fusion = f32[4096,256]{1,0:T(8,128)} fusion(f32[64,256]{1,0:T(8,128)S(1)} %copy.146, s32[4096]{0:T(1024)S(1)} %broadcast_clamp_fusion), kind=kCustom, calls=%fused_computation | custom fusion | bytes 8404992 | tf_op jit(solution)/shard_map/gather | solution.py:82
  79.2 9.2 %copy.147 = f32[64,64,256]{1,0,2:T(8,128)} copy(f32[64,64,256]{2,1,0:T(8,128)} %bitcast.243) | data formatting | bytes 8388608 | tf_op jit(solution)/shard_map/gather | solution.py:82
  88.4 15.4 %fusion.66 = f32[256,4,64]{2,1,0:T(4,128)S(1)} fusion(f32[4,64,256]{1,0,2:T(4,128)S(1)} %copy.148, f32[64,64,256]{1,0,2:T(8,128)} %copy.147, pred[64,64]{1,0:T(8,128)(4,1)S(1)} %subtract_compare_fusion), kind=kOutput, calls=%fused_computation.82 | convolution fusion | flops 51380224 | bytes 4722688 | tf_op jit(solution)/shard_map/abc,nbc->nac/dot_general | solution.py:84
  103.9 2.8 fusion.79
  107.1 29.3 %psum.21 = f32[256]{0:T(256)S(1)} all-reduce(f32[256]{0:T(256)S(1)} %get-tuple-element.913), channel_id=1, replica_groups=mesh['ctx'=16,'tp'=16] {'tp'}, use_global_device_ids=true, to_apply=%region_4.5 | all-reduce | flops 256 | bytes 2048 | tf_op jit(solution)/shard_map/psum | solution.py:178
  141.3 51.2 %all-gather.10.cloned.1.call-done = bf16[4096,256]{1,0:T(8,128)(2,1)} async-done(((bf16[256,256]{1,0:T(8,128)(2,1)}), bf16[4096,256]{1,0:T(8,128)(2,1)}) %all-gather.10.cloned.1.call-update) | async-done | bytes 2097168 | tf_op jit(solution)/shard_map/all_gather | solution.py:194
  192.5 3.9 reshape.219
  196.4 2.0 copy.163
  198.5 49.1 %all-gather.8.cloned.1.call-done = bf16[4096,256]{1,0:T(8,128)(2,1)} async-done(((bf16[256,256]{1,0:T(8,128)(2,1)}), bf16[4096,256]{1,0:T(8,128)(2,1)}) %all-gather.8.cloned.1.call-update) | async-done | bytes 2097168 | tf_op jit(solution)/shard_map/all_gather | solution.py:193
  247.6 4.0 reshape.249
  251.5 3.4 copy.161
  255.0 27.7 %while.67 = (s32[]{:T(128)}, f32[2,256]{1,0:T(2,128)S(1)}, f32[2,256]{1,0:T(2,128)S(1)}, f32[256,2,128]{2,0,1:T(8,128)S(1)}, s32[8]{0:T(128)}, /*index=5*/s32[25...) while((s32[]{:T(128)}, f32[2,256]{1,0:T(2,128)S(1)}, ...), condition=%wide.region_10.11_spmd, body=%wide.region_5.10_spmd.sunk | while | flops 136316928 | bytes 4630295 | solution.py:212
  258.1 2.7 conditional.6
  283.7 1.9 reshape.225
  286.9 50.8 %all_gather.49 = f32[2,4096]{0,1:T(8,128)} all-gather(f32[2,256]{0,1:T(8,128)S(1)} %bitcast.246), channel_id=1, replica_groups=mesh['ctx'=16,'tp'=16] {'ctx'}, dimensions={1}, use_global_device_ids=true | all-gather | bytes 34816 | tf_op jit(solution)/shard_map/all_gather | solution.py:262
  337.8 2.2 copy.172
  340.0 2.6 reshape.250
  342.5 1.7 copy.168
  344.3 23.1 %all_gather.47 = f32[2,4096]{1,0:T(2,128)S(1)} all-gather(f32[2,256]{1,0:T(2,128)S(1)} %log_add_fusion), channel_id=1, replica_groups=mesh['ctx'=16,'tp'=16] {'ctx'}, dimensions={1}, use_global_device_ids=true | all-gather | bytes 34816 | tf_op jit(solution)/shard_map/all_gather | solution.py:261
  367.3 2.5 reshape.251
  369.9 1.7 copy.170
  371.7 86.2 %while.68 = (s32[]{:T(128)}, f32[256,2,128]{2,0,1:T(8,128)S(1)}, f32[256,2,128]{2,0,1:T(8,128)S(1)}, s32[8]{0:T(128)}, s32[256]{0:T(256)S(1)}, /*index=5*/bf16[8...) while((s32[]{:T(128)}, f32[256,2,128]{2,0,1:T(8,128)S(1)}, ...), condition=%wide.region_15.16_spmd, body=%wide.region_12.15_spmd.sunk | while | flops 270598656 | bytes 5799249 | solution.py:295
  376.0 6.5 %conditional.7 = ((f32[256,2,128]{2,0,1:T(8,128)S(1)}, f32[256,2,128]{2,0,1:T(8,128)S(1)})) conditional(s32[]{:T(128)} %bitcast.236, (f32[256,2,128]{2,0,1:T(8,128)S(1)}, f32[256,2,128]{2,0,1:T(8,128)S(1)}) %tuple.175, (s32[512]{0:T(512)S(1)}, s32[256]{0:T(256)S(1)}, bf16[8,512,2,128]{3,1,2,0:T(8,128)(2,1)}, s32[]{:T(128)}, ...), branch_computations={%region_13.13_spmd, %region_14.14_spmd} | conditional | flops 270598144 | bytes 5796926 | solution.py:293
  386.8 6.5 %conditional.7 = ((f32[256,2,128]{2,0,1:T(8,128)S(1)}, f32[256,2,128]{2,0,1:T(8,128)S(1)})) conditional(s32[]{:T(128)} %bitcast.236, (f32[256,2,128]{2,0,1:T(8,128)S(1)}, f32[256,2,128]{2,0,1:T(8,128)S(1)}) %tuple.175, (s32[512]{0:T(512)S(1)}, s32[256]{0:T(256)S(1)}, bf16[8,512,2,128]{3,1,2,0:T(8,128)(2,1)}, s32[]{:T(128)}, ...), branch_computations={%region_13.13_spmd, %region_14.14_spmd} | conditional | flops 270598144 | bytes 5796926 | solution.py:293
  390.3 1.6 fusion.23
  397.6 6.5 %conditional.7 = ((f32[256,2,128]{2,0,1:T(8,128)S(1)}, f32[256,2,128]{2,0,1:T(8,128)S(1)})) conditional(s32[]{:T(128)} %bitcast.236, (f32[256,2,128]{2,0,1:T(8,128)S(1)}, f32[256,2,128]{2,0,1:T(8,128)S(1)}) %tuple.175, (s32[512]{0:T(512)S(1)}, s32[256]{0:T(256)S(1)}, bf16[8,512,2,128]{3,1,2,0:T(8,128)(2,1)}, s32[]{:T(128)}, ...), branch_computations={%region_13.13_spmd, %region_14.14_spmd} | conditional | flops 270598144 | bytes 5796926 | solution.py:293
  401.1 1.6 fusion.23
  408.3 6.5 %conditional.7 = ((f32[256,2,128]{2,0,1:T(8,128)S(1)}, f32[256,2,128]{2,0,1:T(8,128)S(1)})) conditional(s32[]{:T(128)} %bitcast.236, (f32[256,2,128]{2,0,1:T(8,128)S(1)}, f32[256,2,128]{2,0,1:T(8,128)S(1)}) %tuple.175, (s32[512]{0:T(512)S(1)}, s32[256]{0:T(256)S(1)}, bf16[8,512,2,128]{3,1,2,0:T(8,128)(2,1)}, s32[]{:T(128)}, ...), branch_computations={%region_13.13_spmd, %region_14.14_spmd} | conditional | flops 270598144 | bytes 5796926 | solution.py:293
  411.9 1.6 fusion.23
  419.1 6.5 %conditional.7 = ((f32[256,2,128]{2,0,1:T(8,128)S(1)}, f32[256,2,128]{2,0,1:T(8,128)S(1)})) conditional(s32[]{:T(128)} %bitcast.236, (f32[256,2,128]{2,0,1:T(8,128)S(1)}, f32[256,2,128]{2,0,1:T(8,128)S(1)}) %tuple.175, (s32[512]{0:T(512)S(1)}, s32[256]{0:T(256)S(1)}, bf16[8,512,2,128]{3,1,2,0:T(8,128)(2,1)}, s32[]{:T(128)}, ...), branch_computations={%region_13.13_spmd, %region_14.14_spmd} | conditional | flops 270598144 | bytes 5796926 | solution.py:293
  422.6 1.6 fusion.23
  429.9 6.5 %conditional.7 = ((f32[256,2,128]{2,0,1:T(8,128)S(1)}, f32[256,2,128]{2,0,1:T(8,128)S(1)})) conditional(s32[]{:T(128)} %bitcast.236, (f32[256,2,128]{2,0,1:T(8,128)S(1)}, f32[256,2,128]{2,0,1:T(8,128)S(1)}) %tuple.175, (s32[512]{0:T(512)S(1)}, s32[256]{0:T(256)S(1)}, bf16[8,512,2,128]{3,1,2,0:T(8,128)(2,1)}, s32[]{:T(128)}, ...), branch_computations={%region_13.13_spmd, %region_14.14_spmd} | conditional | flops 270598144 | bytes 5796926 | solution.py:293
  433.4 1.6 fusion.23
  440.6 6.5 %conditional.7 = ((f32[256,2,128]{2,0,1:T(8,128)S(1)}, f32[256,2,128]{2,0,1:T(8,128)S(1)})) conditional(s32[]{:T(128)} %bitcast.236, (f32[256,2,128]{2,0,1:T(8,128)S(1)}, f32[256,2,128]{2,0,1:T(8,128)S(1)}) %tuple.175, (s32[512]{0:T(512)S(1)}, s32[256]{0:T(256)S(1)}, bf16[8,512,2,128]{3,1,2,0:T(8,128)(2,1)}, s32[]{:T(128)}, ...), branch_computations={%region_13.13_spmd, %region_14.14_spmd} | conditional | flops 270598144 | bytes 5796926 | solution.py:293
  451.4 6.5 %conditional.7 = ((f32[256,2,128]{2,0,1:T(8,128)S(1)}, f32[256,2,128]{2,0,1:T(8,128)S(1)})) conditional(s32[]{:T(128)} %bitcast.236, (f32[256,2,128]{2,0,1:T(8,128)S(1)}, f32[256,2,128]{2,0,1:T(8,128)S(1)}) %tuple.175, (s32[512]{0:T(512)S(1)}, s32[256]{0:T(256)S(1)}, bf16[8,512,2,128]{3,1,2,0:T(8,128)(2,1)}, s32[]{:T(128)}, ...), branch_computations={%region_13.13_spmd, %region_14.14_spmd} | conditional | flops 270598144 | bytes 5796926 | solution.py:293
  455.0 1.6 fusion.23
  458.2 26.6 %psum.22 = f32[256]{0:T(256)S(1)} all-reduce(f32[256]{0:T(256)S(1)} %get-tuple-element.826), channel_id=1, replica_groups=mesh['ctx'=16,'tp'=16] {'tp'}, use_global_device_ids=true, to_apply=%region_17.18 | all-reduce | flops 256 | bytes 2048 | tf_op jit(solution)/shard_map/psum | solution.py:303
  486.7 3.5 fusion.74
  490.2 16.1 %fusion.64 = f32[256,4,64]{2,1,0:T(4,128)} fusion(f32[4,64,256]{1,0,2:T(4,128)S(1)} %copy.174, f32[64,64,256]{1,0,2:T(8,128)} %copy.147, pred[64,64]{1,0:T(8,128)(4,1)S(1)} %copy-done.19), kind=kOutput, calls=%fused_computation.80 | convolution fusion | flops 51380224 | bytes 4722688 | tf_op jit(solution)/shard_map/abc,nbc->nac/dot_general | solution.py:84
  506.4 28.7 %while.70 = (s32[]{:T(128)}, f32[256,2,128]{2,0,1:T(8,128)S(1)}, s32[8]{0:T(128)}, s32[256]{0:T(256)S(1)}, bf16[8,512,2,128]{3,1,2,0:T(8,128)(2,1)}, /*index=5*/...) while((s32[]{:T(128)}, f32[256,2,128]{2,0,1:T(8,128)S(1)}, ...), condition=%wide.region_25.26_spmd, body=%wide.region_22.25_spmd.sunk | while | flops 203162112 | bytes 3947251 | solution.py:258
  509.5 3.8 conditional.8
  535.4 26.6 %all-gather.2 = bf16[256,256]{1,0:T(8,128)(2,1)S(1)} all-gather(bf16[16,256]{1,0:T(8,128)(2,1)S(1)} %copy.180), channel_id=4, replica_groups=mesh['ctx'=16,'tp'=16] {'ctx'}, dimensions={0}, use_global_device_ids=true | all-gather | bytes 139264 | tf_op jit(solution)/shard_map/all_gather | solution.py:42
  561.9 9.8 %while.69 = (s32[]{:T(128)}, f32[16,256]{1,0:T(8,128)S(1)}, s32[]{:T(128)}, bf16[16,16,256]{2,1,0:T(8,128)(2,1)}, bf16[16,16,256]{2,1,0:T(8,128)(2,1)S(1)}, /*index=5*/s32[]{:T(128)}, s32[]{:T(128)}, s32[]{:T(128)}, s32[]{:T(128)}) while((s32[]{:T(128)}, f32[16,256]{1,0:T(8,128)S(1)}, s32[]{:T(128)}, bf16[16,16,256]{2,1,0:T(8,128)(2,1)}, ...), condition=%wide.region_19.20_spmd, body=%wide.region_18.19_spmd.sunk | while | flops 16390 | bytes 49295 | solution.py:59
  572.4 2.8 fusion.78
  576.4 33.9 %psum.23 = f32[256]{0:T(256)} all-reduce(f32[256]{0:T(256)S(1)} %get-tuple-element.825), channel_id=1, replica_groups=mesh['ctx'=16,'tp'=16] {'ctx'}, use_global_device_ids=true, to_apply=%region_21.22 | all-reduce | flops 256 | bytes 2048 | tf_op jit(solution)/shard_map/psum | solution.py:301
  (320 shorter events, 113.7 us)
Async XLA Ops:
  7.2 185.3 %all-gather.10.cloned.1.call-start = ((), (), s32[]{:S(2)}) async-start(), calls=%async_computation.1 | async-start | bytes 2228224 | tf_op jit(solution)/shard_map/all_gather | solution.py:194
  7.2 2.3 copy-start.33
  7.3 53.1 %copy-start.27 = (f32[4]{0:T(128)}, f32[4]{0:T(128)S(1)}, u32[]{:S(2)}) copy-start(f32[4]{0:T(128)S(1)} %iota_multiply_fusion) | copy-start | bytes 52
  7.3 81.1 %copy-start.18 = (pred[64,64]{1,0:T(8,128)(4,1)}, pred[64,64]{1,0:T(8,128)(4,1)S(1)}, u32[]{:S(2)}) copy-start(pred[64,64]{1,0:T(8,128)(4,1)S(1)} %subtract_compare_fusion) | copy-start | bytes 12292
  7.3 96.5 %copy-start.31 = (f32[64]{0:T(128)}, f32[64]{0:T(128)S(1)}, u32[]{:S(2)}) copy-start(f32[64]{0:T(128)S(1)} %iota_add_fusion.2) | copy-start | bytes 772
  8.2 95.6 %copy-start.4 = (f32[16,256]{0,1:T(8,128)}, f32[16,256]{0,1:T(8,128)S(1)}, u32[]{:S(2)}) copy-start(f32[16,256]{0,1:T(8,128)S(1)} %neg.3) | copy-start | bytes 49156
  9.5 50.8 %copy-start.12 = (f32[16,256]{1,0:T(8,128)}, f32[16,256]{1,0:T(8,128)S(1)}, u32[]{:S(2)}) copy-start(f32[16,256]{1,0:T(8,128)S(1)} %copy.156) | copy-start | bytes 49156
  13.1 48.1 %copy-start.22 = (f32[16,256]{1,0:T(8,128)S(1)}, f32[16,256]{1,0:T(8,128)}, u32[]{:S(2)}) copy-start(f32[16,256]{1,0:T(8,128)} %param.31) | copy-start | bytes 49156
  60.1 0.7 copy-start.11
  60.3 0.5 copy-start.29
  61.3 42.5 %copy-start.14 = (f32[16,256]{0,1:T(8,128)}, f32[16,256]{0,1:T(8,128)S(1)}, u32[]{:S(2)}) copy-start(f32[16,256]{0,1:T(8,128)S(1)} %copy.144) | copy-start | bytes 49156
  103.8 3.1 copy-start.8
  103.8 3.1 copy-start.17
  103.9 32.6 %copy-start.23 = (f32[256]{0:T(256)S(1)}, f32[256]{0:T(256)}, u32[]{:S(2)}) copy-start(f32[256]{0:T(256)} %param.32) | copy-start | bytes 3076
  106.7 32.6 %copy-start.3 = (bf16[256,256]{1,0:T(8,128)(2,1)S(1)}, bf16[256,256]{1,0:T(8,128)(2,1)}, u32[]{:S(2)}) copy-start(bf16[256,256]{1,0:T(8,128)(2,1)} %param.33) | copy-start | bytes 393220
  106.7 32.7 %copy-start.1 = (bf16[256,256]{1,0:T(8,128)(2,1)S(1)}, bf16[256,256]{1,0:T(8,128)(2,1)}, u32[]{:S(2)}) copy-start(bf16[256,256]{1,0:T(8,128)(2,1)} %param.35) | copy-start | bytes 393220
  106.7 32.8 %copy-start.2 = (bf16[256,256]{1,0:T(8,128)(2,1)S(1)}, bf16[256,256]{1,0:T(8,128)(2,1)}, u32[]{:S(2)}) copy-start(bf16[256,256]{1,0:T(8,128)(2,1)} %param.34) | copy-start | bytes 393220
  136.5 60.0 %copy-start.20 = (f32[256]{0:T(256)}, f32[256]{0:T(256)S(1)}, u32[]{:S(2)}) copy-start(f32[256]{0:T(256)S(1)} %add_rsqrt_fusion) | copy-start | bytes 3076
  137.3 110.3 %all-gather.8.cloned.1.call-start = ((), (), s32[]{:S(2)}) async-start(), calls=%async_computation | async-start | bytes 2228224 | tf_op jit(solution)/shard_map/all_gather | solution.py:193
  138.0 201.9 %all-gather.12.cloned.1.call-start = ((), (), s32[]{:S(2)}) async-start(), calls=%async_computation.2 | async-start | bytes 2228224 | tf_op jit(solution)/shard_map/all_gather | solution.py:265
  138.8 228.6 %all-gather.14.cloned.1.call-start = ((), (), s32[]{:S(2)}) async-start(), calls=%async_computation.3 | async-start | bytes 2228224 | tf_op jit(solution)/shard_map/all_gather | solution.py:266
  282.7 57.3 %copy-start = (bf16[8,512,2,128]{3,1,2,0:T(8,128)(2,1)}, bf16[8,512,2,128]{3,1,2,0:T(8,128)(2,1)S(1)}, u32[]{:S(2)}) copy-start(bf16[8,512,2,128]{3,1,2,0:T(8,128)(2,1)S(1)} %get-tuple-element.1361) | copy-start | bytes 6291460
  344.3 25.6 %copy-start.25 = (f32[2,256]{1,0:T(2,128)}, f32[2,256]{1,0:T(2,128)S(1)}, u32[]{:S(2)}) copy-start(f32[2,256]{1,0:T(2,128)S(1)} %log_add_fusion) | copy-start | bytes 6148
  369.9 1.8 copy-start.16
  371.7 86.3 %copy-start.21 = (f32[256]{0:T(256)S(1)}, f32[256]{0:T(256)}, u32[]{:S(2)}) copy-start(f32[256]{0:T(256)} %copy-done.20) | copy-start | bytes 3076
  371.7 86.3 %copy-start.24 = (f32[256]{0:T(256)S(1)}, f32[256]{0:T(256)}, u32[]{:S(2)}) copy-start(f32[256]{0:T(256)} %param.32) | copy-start | bytes 3076
  371.7 113.9 %copy-start.9 = (bf16[256,256]{1,0:T(8,128)(2,1)S(1)}, bf16[256,256]{1,0:T(8,128)(2,1)}, u32[]{:S(2)}) copy-start(bf16[256,256]{1,0:T(8,128)(2,1)} %param.26) | copy-start | bytes 393220
  457.9 28.7 %copy-start.5 = (f32[16,256]{0,1:T(8,128)S(1)}, f32[16,256]{0,1:T(8,128)}, u32[]{:S(2)}) copy-start(f32[16,256]{0,1:T(8,128)} %copy-done.4) | copy-start | bytes 49156
  457.9 28.7 %copy-start.34 = (f32[64]{0:T(128)S(1)}, f32[64]{0:T(128)}, u32[]{:S(2)}) copy-start(f32[64]{0:T(128)} %copy-done.33) | copy-start | bytes 772
  485.6 4.6 copy-start.19
  490.2 16.2 %copy-start.26 = (f32[2,256]{1,0:T(2,128)S(1)}, f32[2,256]{1,0:T(2,128)}, u32[]{:S(2)}) copy-start(f32[2,256]{1,0:T(2,128)} %copy-done.25) | copy-start | bytes 6148
  535.1 36.8 %copy-start.13 = (f32[16,256]{1,0:T(8,128)S(1)}, f32[16,256]{1,0:T(8,128)}, u32[]{:S(2)}) copy-start(f32[16,256]{1,0:T(8,128)} %copy-done.12) | copy-start | bytes 49156
  535.1 36.8 %copy-start.28 = (f32[4]{0:T(128)S(1)}, f32[4]{0:T(128)}, u32[]{:S(2)}) copy-start(f32[4]{0:T(128)} %copy-done.27) | copy-start | bytes 52
  535.1 36.8 %copy-start.30 = (f32[4]{0:T(128)S(1)}, f32[4]{0:T(128)}, u32[]{:S(2)}) copy-start(f32[4]{0:T(128)} %copy-done.29) | copy-start | bytes 52
  535.2 37.2 %copy-start.10 = (f32[256,4,64]{2,1,0:T(4,128)S(1)}, f32[256,4,64]{2,1,0:T(4,128)}, u32[]{:S(2)}) copy-start(f32[256,4,64]{2,1,0:T(4,128)} %fusion.64) | copy-start | bytes 786436
  535.2 37.2 %copy-start.15 = (f32[16,256]{0,1:T(8,128)S(1)}, f32[16,256]{0,1:T(8,128)}, u32[]{:S(2)}) copy-start(f32[16,256]{0,1:T(8,128)} %copy-done.14) | copy-start | bytes 49156
  535.2 37.2 %copy-start.32 = (f32[64]{0:T(128)S(1)}, f32[64]{0:T(128)}, u32[]{:S(2)}) copy-start(f32[64]{0:T(128)} %copy-done.31) | copy-start | bytes 772
  572.4 3.2 copy-start.6
  572.4 3.2 copy-start.7
Sparse Core Ops, SparseCore 0:
  137.4 55.0 all-gather.9
  195.2 52.3 all-gather.7
  250.3 52.3 all-gather.11
  305.2 54.7 all-gather.13
where the time goes:
time: 621 us; the launch traced here: 618 us
  blocking collectives  236 us (38%)
  local copies, waits for them, and re-layouts  105 us (17%)
  waiting for transfers between devices  102 us (16%)
  matrix products  83.2 us (13%)
  loops' own time  48.4 us (8%)
  other arithmetic  28.2 us (5%)
  between operations  14.5 us (2%)
    all_gather x1, waiting for transfers between devices, on_device(): vals_piece = lax.all_gather(values, 'ctx', axis=0, tiled=True)  51.2 us
    all_gather x1, blocking collectives, on_device(): lax.all_gather(delta, 'ctx', axis=1, tiled=True)  50.8 us
    all_gather x1, waiting for transfers between devices, on_device(): keys_piece = lax.all_gather(key_att, 'ctx', axis=0, tiled=True)  49.1 us
    all_gather x2, blocking collectives, entering_2(): lax.all_gather(part.astype(kind), axis)  45.8 us
    psum x1, blocking collectives, on_device(): gain_grad = lax.psum(jnp.sum(dvalues * normed, axis=0), 'ctx')  33.9 us
    dot_general x2, matrix products, modal_local(): inner = jnp.einsum('abc,nbc->nac', toeplitz, blocks, precision=HIGHEST)  31.5 us
    psum x1, blocking collectives, on_device(): squares = lax.psum(jnp.sum(summed * summed, axis=1), 'tp')  29.3 us
    dynamic_slice x24, local copies, waits for them, and re-layouts, on_device(): lax.scan(forward_visit, running, (key_blocks, val_blocks, block_starts))  28.9 us
  transfers between devices with their start and end apart: 4, of which 2 were waited for; matrix products, arithmetic and copies ran while one was open for 7% of the time, Pallas kernels for 0%

commit v1 on v0

v1 whole, which is shorter than its diff:
```python
import jax
import jax.numpy as jnp
from jax import lax
from jax.experimental import pallas as pl
from jax.experimental.pallas import tpu as pltpu
from jax.sharding import PartitionSpec as P

HD = 128
BLK = 256
MODES = 16
CHUNK = 64
NX = 4
FILL = -1e30
EPS = 1e-06
LOG2E = 1.4426950408889634
NT = (((1,), (1,)), ((), ()))
HIGHEST = lax.Precision.HIGHEST
F32 = jnp.float32
BF16 = jnp.bfloat16
Q, DO, K, V = 0, 1, 2, 3
R_DV, R_DK, R_ATT, R_DQ = 0, 1, 2, 3


def remote(src, dst, send, recv, **where):
    return pltpu.make_async_remote_copy(
        src_ref=src,
        dst_ref=dst,
        send_sem=send,
        recv_sem=recv,
        device_id=where,
        device_id_type=pl.DeviceIdType.MESH,
    )


def loop(lo, hi, body):
    def step(i, carry):
        body(i)
        return carry

    lax.fori_loop(lo, hi, step, 0)


def halves(row):
    return jnp.concatenate(
        [jnp.broadcast_to(row[:, :HD], (4, HD)), jnp.broadcast_to(row[:, HD:], (4, HD))], axis=0
    )


def columns(row):
    return jnp.transpose(jnp.broadcast_to(row, (HD, row.shape[1])))


def row_sums(x):
    ones = jnp.ones((8, x.shape[1]), F32)
    return lax.dot_general(ones, x, NT, precision=HIGHEST, preferred_element_type=F32)[0:1]


def dot_nt(a, b):
    return lax.dot_general(a, b, NT, preferred_element_type=F32)


def dot(a, b):
    return jnp.dot(a, b, preferred_element_type=F32)


def kernel(
    n_ctx,
    n_tp,
    gate,
    keyp,
    valp,
    stream,
    decay,
    residue,
    gain,
    query,
    key,
    grad,
    att_o,
    gate_o,
    keyp_o,
    valp_o,
    stream_o,
    gain_o,
    query_o,
    key_o,
    xs,
    conv,
    fac,
    res,
    d64,
    up,
    down,
    ends,
    state_out,
    state_in,
    ein,
    tp_out,
    tp_in,
    gain_out,
    gain_in,
    normed,
    inv,
    dsum,
    swap,
    big,
    exps,
    work,
    dprob,
    rel,
    ml,
    dl,
    fs,
    dos,
    qs,
    ls,
    lcol,
    ret_out,
    ret_in,
    st_s,
    st_r,
    tp_s,
    tp_r,
    ga_s,
    ga_r,
    sw_s,
    sw_r,
    bg_s,
    bg_r,
    ml_s,
    ml_r,
    dl_s,
    dl_r,
    ls_s,
    ls_r,
    rt_s,
    rt_r,
):
    b = lax.axis_index("ctx")
    tp = lax.axis_index("tp")
    x = b // 4
    y = (b // 2) % 2
    a = b % 2
    mine = b % 4
    sibling = b + 1 - 2 * a
    across = b + 2 - 4 * y
    scale = HD**-0.5

    barrier = pltpu.get_barrier_semaphore()

    def greet_ctx(r):
        pl.semaphore_signal(
            barrier, 1, device_id={"ctx": lax.rem(b + r, n_ctx)}, device_id_type=pl.DeviceIdType.MESH
        )

    def greet_tp(r):
        pl.semaphore_signal(
            barrier, 1, device_id={"tp": lax.rem(tp + r, n_tp)}, device_id_type=pl.DeviceIdType.MESH
        )

    loop(1, n_ctx, greet_ctx)
    loop(1, n_tp, greet_tp)

    chunk_id = lax.broadcasted_iota(jnp.int32, (8, HD), 0) % 4
    chunk_f = chunk_id.astype(F32)
    for m in range(MODES):
        rate = halves(decay[m : m + 1, :])
        fac[m] = jnp.exp(-rate)
        res[m] = halves(residue[m : m + 1, :])
        d64[m] = jnp.exp(-CHUNK * rate)
        up[m] = jnp.exp(-CHUNK * rate * chunk_f)
        down[m] = jnp.exp(-CHUNK * rate * (3.0 - chunk_f))
    d256 = jnp.exp(-float(BLK) * decay[...])

    def filter_ends(backward):
        factors = [fac[m] for m in range(MODES)]

        def step(t, states):
            at = CHUNK - 1 - t if backward else t
            column = xs[pl.ds(at, 8, stride=CHUNK), :]
            return tuple(f * s + column for f, s in zip(factors, states))

        zero = jnp.zeros((8, HD), F32)
        states = lax.fori_loop(0, CHUNK, step, (zero,) * MODES, unroll=4)
        weight = up if backward else down
        for m in range(MODES):
            ends[m] = states[m]
            part = states[m] * weight[m]
            ein[m : m + 1, 0:HD] = jnp.sum(part[0:4], axis=0, keepdims=True)
            ein[m : m + 1, HD : 2 * HD] = jnp.sum(part[4:8], axis=0, keepdims=True)
        state_out[int(backward)] = ein[...].astype(BF16)

    def filter_run(backward):
        factors = [fac[m] for m in range(MODES)]
        weights = [res[m] for m in range(MODES)]
        reach = down if backward else up
        entries = []
        for m in range(MODES):
            end = ends[m]
            total = reach[m] * halves(ein[m : m + 1, :])
            power = jnp.ones((8, HD), F32)
            for back in (1, 2, 3):
                moved = pltpu.roll(end, 8 - back if backward else back, 0)
                ok = chunk_id <= 3 - back if backward else chunk_id >= back
                total = total + power * jnp.where(ok, moved, 0.0)
                power = power * d64[m]
            entries.append(total)

        def step(t, states):
            at = CHUNK - 1 - t if backward else t
            column = xs[pl.ds(at, 8, stride=CHUNK), :]
            states = tuple(f * s + column for f, s in zip(factors, states))
            terms = [w * s for w, s in zip(weights, states)]
            while len(terms) > 1:
                terms = [u + v for u, v in zip(terms[::2], terms[1::2])]
            conv[pl.ds(at, 8, stride=CHUNK), :] = terms[0]
            return states

        lax.fori_loop(0, CHUNK, step, tuple(entries), unroll=2)

    def state_copy(way, dst):
        return remote(
            state_out.at[way], state_in.at[way, b], st_s.at[way, dst], st_r.at[way, b], ctx=dst
        )

    def state_wait(way, src):
        remote(
            state_out.at[way], state_in.at[way, src], st_s.at[way, src], st_r.at[way, src], ctx=src
        ).wait_recv()

    mixed = keyp[...].astype(F32) * valp[...].astype(F32)
    xs[0:BLK, :] = mixed[:, :HD]
    xs[BLK:, :] = mixed[:, HD:]
    filter_ends(False)

    def place(t, array):
        big[t, x, y] = array[:, pl.ds(pl.multiple_of(y * HD, HD), HD)]
        swap[t] = array[:, pl.ds(pl.multiple_of((1 - y) * HD, HD), HD)]

    def swap_copy(t):
        return remote(swap.at[t], big.at[t, x, y], sw_s.at[t], sw_r.at[t], ctx=across)

    def swap_wait(t):
        remote(swap.at[t], big.at[t, x, 1 - y], sw_s.at[t], sw_r.at[t], ctx=across).wait_recv()

    def x_copy(t, piece, to):
        return remote(
            big.at[t, x, piece],
            big.at[t, x, piece],
            bg_s.at[t, piece, to],
            bg_r.at[t, piece, x],
            ctx=4 * to + mine,
        )

    def sib_copy(t, piece):
        return remote(
            big.at[t, x, piece],
            big.at[t, 4, piece],
            bg_s.at[t, piece, x],
            bg_r.at[t, piece, 4],
            ctx=sibling,
        )

    def piece_wait(t, piece, slot):
        remote(
            big.at[t, x, piece],
            big.at[t, slot, piece],
            bg_s.at[t, piece, slot % 4],
            bg_r.at[t, piece, slot],
            ctx=sibling,
        ).wait_recv()

    def targets(t, body):
        if t in (Q, DO):
            loop(0, x, lambda i: body(x - 1 - i))
        else:
            loop(x + 1, NX, body)

    def send_piece(t, piece):
        sib_copy(t, piece).start()
        targets(t, lambda to: x_copy(t, piece, to).start())

    def drain_piece(t, piece):
        sib_copy(t, piece).wait_send()
        targets(t, lambda to: x_copy(t, piece, to).wait_send())

    place(Q, query)
    place(DO, grad)
    place(K, key)
    rel[...] = (
        lax.broadcasted_iota(jnp.int32, (BLK, 2 * BLK), 1)
        + BLK * (lax.broadcasted_iota(jnp.int32, (BLK, 2 * BLK), 1) // BLK)
        + BLK * a
        - lax.broadcasted_iota(jnp.int32, (BLK, 2 * BLK), 0)
    )

    pl.semaphore_wait(barrier, n_ctx + n_tp - 2)

    loop(b + 1, n_ctx, lambda dst: state_copy(0, dst).start())
    for t in (Q, DO, K):
        swap_copy(t).start()
    for t in (Q, DO, K):
        send_piece(t, y)
    swap_wait(Q)
    send_piece(Q, 1 - y)

    def gather_states(way):
        def hop(i, total):
            src = n_ctx - 1 - i if way else i
            state_wait(way, src)
            return d256 * total + state_in[way, src].astype(F32)

        count = n_ctx - 1 - b if way else b
        ein[...] = lax.fori_loop(0, count, hop, jnp.zeros((MODES, 2 * HD), F32))

    def tp_copy(which, r):
        return remote(
            tp_out.at[which],
            tp_in.at[which, n_tp - 1 - r],
            tp_s.at[which],
            tp_r.at[which],
            tp=lax.rem(tp + r, n_tp),
        )

    def tp_all(which):
        return remote(
            tp_in.at[which], tp_in.at[which], tp_s.at[which], tp_r.at[which], tp=lax.rem(tp + 1, n_tp)
        )

    gather_states(0)
    filter_run(False)
    total = stream[...].astype(F32) + gate[...].astype(F32) * jnp.concatenate(
        [conv[0:BLK, :], conv[BLK:, :]], axis=1
    )
    normed[...] = total
    tp_out[0] = row_sums(total * total)
    loop(1, n_tp, lambda r: tp_copy(0, r).start())

    for t in (DO, K):
        swap_wait(t)
        send_piece(t, 1 - y)

    def chip_tile(t, r):
        return big[t, jnp.where(r % 2 == a, x, 4), r // 2]

    def x_tile(t, slot):
        return big[t, slot].reshape(2 * BLK, HD)

    neg = jnp.full((4, 2 * BLK), FILL, F32)
    ml[x, 0:4] = neg
    ml[x, 4:8] = jnp.zeros_like(neg)

    def key_scores(xq):
        def tile(r, top):
            s = dot_nt(chip_tile(K, r), x_tile(Q, xq)) * (scale * LOG2E)
            s = jnp.where(rel[...] >= BLK * r - 4 * BLK * (xq - x), s, FILL)
            work[r] = s
            return jnp.maximum(top, jnp.max(s, axis=0, keepdims=True))

        top = lax.fori_loop(0, 4, tile, jnp.full((1, 2 * BLK), FILL, F32))

        def tile_exp(r, total):
            e = jnp.exp2(work[r] - top)
            exps[xq, r] = e.astype(BF16)
            return total + jnp.sum(e, axis=0, keepdims=True)

        total = lax.fori_loop(0, 4, tile_exp, jnp.zeros((1, 2 * BLK), F32))
        ml[x, pl.ds(xq, 1)] = top
        ml[x, pl.ds(4 + xq, 1)] = total

    for piece in (0, 1):
        piece_wait(K, piece, 4)
    key_scores(x)

    def tp_total(which):
        tp_all(which).wait_recv()
        return jnp.sum(tp_in[which], axis=0) + tp_out[which]

    inverse = columns(lax.rsqrt(tp_total(0) / float(n_tp * 2 * HD) + EPS))
    inv[...] = inverse
    normed[...] = normed[...] * jnp.concatenate([inverse, inverse], axis=1)
    swap[V] = jnp.zeros((BLK, HD), BF16)
    vals = (normed[...] * gain[...]).astype(BF16)

    @pl.when(y == 0)
    def _():
        big[V, x, 0] = vals[:, :HD]
        swap[V] = vals[:, HD:]

    @pl.when(y == 1)
    def _():
        big[V, x, 1] = vals[:, HD:]
        swap[V] = vals[:, :HD]

    swap_copy(V).start()
    send_piece(V, y)

    def later_scores(xq):
        for piece in (0, 1):
            piece_wait(Q, piece, xq)
        key_scores(xq)

    loop(x + 1, NX, later_scores)
    swap_wait(V)
    send_piece(V, 1 - y)

    def stat_copy(buf, send, recv, to):
        return remote(buf.at[x], buf.at[x], send.at[to], recv.at[x], ctx=4 * to + mine)

    def stat_wait(buf, send, recv, src):
        remote(buf.at[src], buf.at[src], send.at[src], recv.at[src], ctx=4 * src + mine).wait_recv()

    def others(body):
        loop(1, NX, lambda r: body(lax.rem(x + r, NX)))

    others(lambda to: stat_copy(ml, ml_s, ml_r, to).start())
    others(lambda src: stat_wait(ml, ml_s, ml_r, src))
    tops = jnp.max(ml[:, 0:4, :], axis=0)
    sums = jnp.sum(ml[:, 4:8, :] * jnp.exp2(ml[:, 0:4, :] - tops[None]), axis=0)
    lse = tops + jnp.log2(sums)
    fs[4:8] = lse
    fs[0:4] = jnp.exp2(ml[x, 0:4] - lse)

    def sib_stat(kind):
        return remote(ls.at[kind, 0], ls.at[kind, 1], ls_s.at[kind], ls_r.at[kind], ctx=sibling)

    ls[0, 0] = fs[pl.ds(4 + x, 1)]
    sib_stat(0).start()

    def scale_rows(xq):
        f = columns(fs[pl.ds(xq, 1)])
        dos[xq] = (x_tile(DO, xq).astype(F32) * f).astype(BF16)
        qs[xq] = (x_tile(Q, xq).astype(F32) * (f * scale)).astype(BF16)

    def later_rows(xq):
        for piece in (0, 1):
            piece_wait(DO, piece, xq)
        scale_rows(xq)

    scale_rows(x)
    loop(x + 1, NX, later_rows)

    def ret_copy(t, r):
        return remote(
            ret_out.at[t, r], ret_in.at[t, mine], rt_s.at[t, r], rt_r.at[t, mine], ctx=4 * x + r
        )

    def ret_wait(t, src):
        remote(
            ret_out.at[t, src], ret_in.at[t, src], rt_s.at[t, src], rt_r.at[t, src], ctx=4 * x + src
        ).wait_recv()

    def quad(body):
        loop(1, 4, lambda i: body(lax.rem(mine + i, 4)))

    def give_back(t, r, value):
        ret_out[t, r] = value.astype(BF16)

        @pl.when(r != mine)
        def _():
            ret_copy(t, r).start()

        @pl.when(r == mine)
        def _():
            ret_in[t, mine] = ret_out[t, mine]

    def take_back(t):
        quad(lambda src: ret_wait(t, src))
        return jnp.concatenate(
            [
                ret_in[t, 0].astype(F32) + ret_in[t, 1].astype(F32),
                ret_in[t, 2].astype(F32) + ret_in[t, 3].astype(F32),
            ],
            axis=1,
        )

    zero_tile = jnp.zeros((BLK, HD), F32)

    def value_grads(r):
        total = lax.fori_loop(
            x, NX, lambda xq, acc: acc + dot(exps[xq, r], dos[xq]), zero_tile
        )
        give_back(R_DV, r, total)

    loop(0, 4, value_grads)

    for piece in (0, 1):
        piece_wait(V, piece, 4)
    dl[x] = jnp.zeros((8, 2 * BLK), F32)

    def key_delta(xq):
        def tile(r, total):
            dp = dot_nt(chip_tile(V, r), x_tile(DO, xq))
            dprob[xq, r] = dp
            return total + jnp.sum(exps[xq, r].astype(F32) * dp, axis=0, keepdims=True)

        total = lax.fori_loop(0, 4, tile, jnp.zeros((1, 2 * BLK), F32))
        dl[x, pl.ds(xq, 1)] = total * fs[pl.ds(xq, 1)]

    loop(x, NX, key_delta)
    others(lambda to: stat_copy(dl, dl_s, dl_r, to).start())

    dvalues = take_back(R_DV)
    dsum[...] = dvalues * gain[...]
    tp_out[1] = row_sums(dsum[...] * normed[...])
    loop(1, n_tp, lambda r: tp_copy(1, r).start())
    gain_out[...] = jnp.sum(dvalues * normed[...], axis=0, keepdims=True)

    def gain_copy(r):
        return remote(
            gain_out, gain_in.at[n_ctx - 1 - r], ga_s.at[0], ga_r.at[0], ctx=lax.rem(b + r, n_ctx)
        )

    loop(1, n_ctx, lambda r: gain_copy(r).start())

    others(lambda src: stat_wait(dl, dl_s, dl_r, src))
    fs[0:8] = jnp.sum(dl[...], axis=0)
    ls[1, 0] = fs[pl.ds(x, 1)]
    sib_stat(1).start()

    dot_col = columns(tp_total(1) / float(n_tp * 2 * HD))
    inverse2 = jnp.concatenate([inv[...], inv[...]], axis=1)
    dsummed = inverse2 * (dsum[...] - normed[...] * jnp.concatenate([dot_col, dot_col], axis=1))
    stream_o[...] = dsummed.astype(BF16)
    gate_o[...] = (
        dsummed * jnp.concatenate([conv[0:BLK, :], conv[BLK:, :]], axis=1)
    ).astype(BF16)
    back = dsummed * gate[...].astype(F32)
    xs[0:BLK, :] = back[:, :HD]
    xs[BLK:, :] = back[:, HD:]
    filter_ends(True)
    loop(0, b, lambda dst: state_copy(1, dst).start())

    def key_grads(r):
        def add(xq, acc):
            ds = exps[xq, r].astype(F32) * (dprob[xq, r] - fs[pl.ds(xq, 1)])
            return acc + dot(ds.astype(BF16), qs[xq])

        give_back(R_DK, r, lax.fori_loop(x, NX, add, zero_tile))

    loop(0, 4, key_grads)

    gather_states(1)
    filter_run(True)
    dmixed = jnp.concatenate([conv[0:BLK, :], conv[BLK:, :]], axis=1)
    keyp_o[...] = (dmixed * valp[...].astype(F32)).astype(BF16)
    valp_o[...] = (dmixed * keyp[...].astype(F32)).astype(BF16)

    for kind in (0, 1):
        sib_stat(kind).wait_recv()
        for who in (0, 1):
            lcol[kind, who] = columns(ls[kind, who]).reshape(2, BLK, HD)
    for t in (Q, DO):
        for piece in (0, 1):
            piece_wait(t, piece, 4)

    def earlier_wait(src):
        for t in (K, V):
            for piece in (0, 1):
                piece_wait(t, piece, src)

    loop(0, x, earlier_wait)

    def wide(col):
        return jnp.concatenate([col] * 4, axis=1)

    def query_rows(r):
        who = jnp.where(r % 2 == a, 0, 1)

        def add(xk, acc):
            att, dq = acc
            s = dot_nt(chip_tile(Q, r), x_tile(K, xk)) * (scale * LOG2E)
            p = jnp.exp2(s - wide(lcol[0, who, r // 2]))
            p = jnp.where(rel[...] <= BLK * r + 4 * BLK * (x - xk), p, 0.0)
            dp = dot_nt(chip_tile(DO, r), x_tile(V, xk))
            ds = p * (dp - wide(lcol[1, who, r // 2]))
            return (
                att + dot(p.astype(BF16), x_tile(V, xk)),
                dq + dot(ds.astype(BF16), x_tile(K, xk)),
            )

        att, dq = lax.fori_loop(0, x + 1, add, (zero_tile, zero_tile))
        give_back(R_ATT, r, att)
        give_back(R_DQ, r, dq * scale)

    loop(0, 4, query_rows)

    remote(gain_in, gain_in, ga_s.at[0], ga_r.at[0], ctx=sibling).wait_recv()
    gain_o[...] = jnp.sum(gain_in[...], axis=0) + gain_out[...]
    key_o[...] = take_back(R_DK).astype(BF16)
    att_o[...] = take_back(R_ATT).astype(BF16)
    query_o[...] = take_back(R_DQ).astype(BF16)

    loop(b + 1, n_ctx, lambda dst: state_copy(0, dst).wait_send())
    loop(0, b, lambda dst: state_copy(1, dst).wait_send())
    for t in (Q, DO, K, V):
        swap_copy(t).wait_send()
        for piece in (0, 1):
            drain_piece(t, piece)
    for which in (0, 1):
        tp_all(which).wait_send()
        sib_stat(which).wait_send()
    remote(gain_in, gain_in, ga_s.at[0], ga_r.at[0], ctx=sibling).wait_send()
    others(lambda to: stat_copy(ml, ml_s, ml_r, to).wait_send())
    others(lambda to: stat_copy(dl, dl_s, dl_r, to).wait_send())
    for t in (R_DV, R_DK, R_ATT, R_DQ):
        quad(lambda r: ret_copy(t, r).wait_send())


def on_device(n_ctx, n_tp, *arrays):
    (gate, keyp, valp, stream, decay, residue, gain, query, key, grad) = arrays
    rows, chans = stream.shape
    vmem = pl.BlockSpec(memory_space=pltpu.VMEM)
    full = jax.ShapeDtypeStruct((rows, chans), BF16)
    dma = pltpu.SemaphoreType.DMA

    def body(*refs):
        kernel(n_ctx, n_tp, *refs)

    scratch = [
        pltpu.VMEM((2 * BLK, HD), F32),
        pltpu.VMEM((2 * BLK, HD), F32),
        *[pltpu.VMEM((MODES, 8, HD), F32)] * 6,
        pltpu.VMEM((2, MODES, 2 * HD), BF16),
        pltpu.VMEM((2, n_ctx, MODES, 2 * HD), BF16),
        pltpu.VMEM((MODES, 2 * HD), F32),
        pltpu.VMEM((2, 1, BLK), F32),
        pltpu.VMEM((2, n_tp - 1, 1, BLK), F32),
        pltpu.VMEM((1, 2 * HD), F32),
        pltpu.VMEM((n_ctx - 1, 1, 2 * HD), F32),
        pltpu.VMEM((BLK, 2 * HD), F32),
        pltpu.VMEM((BLK, HD), F32),
        pltpu.VMEM((BLK, 2 * HD), F32),
        pltpu.VMEM((4, BLK, HD), BF16),
        pltpu.VMEM((4, 5, 2, BLK, HD), BF16),
        pltpu.VMEM((NX, 4, BLK, 2 * BLK), BF16),
        pltpu.VMEM((4, BLK, 2 * BLK), F32),
        pltpu.VMEM((NX, 4, BLK, 2 * BLK), F32),
        pltpu.VMEM((BLK, 2 * BLK), jnp.int32),
        pltpu.VMEM((NX, 8, 2 * BLK), F32),
        pltpu.VMEM((NX, 8, 2 * BLK), F32),
        pltpu.VMEM((8, 2 * BLK), F32),
        pltpu.VMEM((NX, 2 * BLK, HD), BF16),
        pltpu.VMEM((NX, 2 * BLK, HD), BF16),
        pltpu.VMEM((2, 2, 1, 2 * BLK), F32),
        pltpu.VMEM((2, 2, 2, BLK, HD), F32),
        pltpu.VMEM((4, 4, BLK, HD), BF16),
        pltpu.VMEM((4, 4, BLK, HD), BF16),
        dma((2, n_ctx)),
        dma((2, n_ctx)),
        dma((2,)),
        dma((2,)),
        dma((1,)),
        dma((1,)),
        dma((4,)),
        dma((4,)),
        dma((4, 2, 4)),
        dma((4, 2, 5)),
        dma((NX,)),
        dma((NX,)),
        dma((NX,)),
        dma((NX,)),
        dma((2,)),
        dma((2,)),
        dma((4, 4)),
        dma((4, 4)),
    ]
    outs = pl.pallas_call(
        body,
        out_shape=(full,) * 5 + (jax.ShapeDtypeStruct((1, chans), F32),) + (full,) * 2,
        in_specs=[vmem] * 10,
        out_specs=(vmem,) * 8,
        scratch_shapes=scratch,
        compiler_params=pltpu.CompilerParams(
            collective_id=0, has_side_effects=True, vmem_limit_bytes=48 * 1024 * 1024
        ),
    )(gate, keyp, valp, stream, decay, residue, gain.reshape(1, chans), query, key, grad)
    return outs[:5] + (outs[5].reshape(chans),) + outs[6:]


def solution(mesh):
    n_ctx, n_tp = mesh.shape["ctx"], mesh.shape["tp"]
    both = P("ctx", "tp")

    def body(*arrays):
        return on_device(n_ctx, n_tp, *arrays)

    return jax.shard_map(
        body,
        mesh=mesh,
        in_specs=(both,) * 4 + (P(None, "tp"), P(None, "tp"), P("tp")) + (both,) * 3,
        out_specs=(both,) * 5 + (P("tp"),) + (both,) * 2,
        check_vma=False,
    )
```

time: 621 us -> 76 us (0.12)
  blocking collectives: 236 us -> 0 us
  waiting for transfers between devices: 102 us -> 0 us
  local copies, waits for them, and re-layouts: 105 us -> 13.6 us
  matrix products: 83.2 us -> 0 us
  Pallas kernels: 0 us -> 61.3 us
  loops' own time: 48.4 us -> 0 us
  other arithmetic: 28.2 us -> 0 us
  between operations: 14.5 us -> 0.67 us
    all_gather x5 -> x0, blocking collectives: 146 us -> none  [the longest x1 50.8 us: on_device(): lax.all_gather(delta, 'ctx', axis=1, tiled=True)]
    all_gather x4 -> x0, waiting for transfers between devices: 100 us -> none  [the longest x1 51.2 us: on_device(): vals_piece = lax.all_gather(values, 'ctx', axis=0, tiled=True)]
    psum x3 -> x0, blocking collectives: 89.9 us -> none  [the longest x1 33.9 us: on_device(): gain_grad = lax.psum(jnp.sum(dvalues * normed, axis=0), 'ctx')]
    dot_general x34 -> x0, matrix products: 83.2 us -> none  [the longest x2 31.5 us: modal_local(): inner = jnp.einsum('abc,nbc->nac', toeplitz, blocks, precision=HIGHEST)]
    pallas_call x0 -> x1, Pallas kernels: none -> 61.3 us  [on_device(): pl.pallas_call(body, out_shape=(full,) * 5 + (jax.ShapeDtypeStruct((1, ch...]
    another operation x29 -> x0, loops' own time: 48.4 us -> none  [the longest x8 15.9 us: key_visit(): lax.cond(pos_blk[-1] >= query_pos[0], key_work, unchanged, acc_pair)]
    dynamic_slice x32 -> x0, local copies, waits for them, and re-layouts: 29.5 us -> none  [the longest x24 28.9 us: on_device(): lax.scan(forward_visit, running, (key_blocks, val_blocks, block_starts))]
    gather x2 -> x0, local copies, waits for them, and re-layouts: 25.3 us -> none  [modal_local(): kernel[jnp.maximum(lag_index, 0)]]
  transfers between devices with their start and end apart: 4 -> 0, of which waited for: 2 -> 0; matrix products, arithmetic and copies ran while one was open for 7% -> 0% of each run, Pallas kernels for 0% -> 0%
where the time goes in v1:
time: 76 us; the launch traced here: 75.5 us
  Pallas kernels  61.3 us (81%)
  local copies, waits for them, and re-layouts  13.6 us (18%)
    pallas_call x1, Pallas kernels, on_device(): pl.pallas_call(body, out_shape=(full,) * 5 + (jax.ShapeDtypeStruct((1, ch...  61.3 us
    unnamed x28, local copies, waits for them, and re-layouts  13.6 us

profile of v1, /device:TPU:1, one launch (start us, length us, event | category | flops | bytes accessed | tf_op | source)
XLA Modules:
  0.0 75.5 jit_solution(18424291148197765036)
XLA Ops:
  0.6 0.0 copy-start.9
  0.6 0.7 copy-done.9
  1.3 0.0 copy-start
  1.3 0.9 %copy-done = bf16[256,256]{1,0:T(8,128)(2,1)S(1)} copy-done((bf16[256,256]{1,0:T(8,128)(2,1)S(1)}, bf16[256,256]{1,0:T(8,128)(2,1)}, u32[]{:S(2)}) %copy-start) | copy-done | bytes 131096
  2.2 0.0 copy-start.1
  2.2 0.9 %copy-done.1 = bf16[256,256]{1,0:T(8,128)(2,1)S(1)} copy-done((bf16[256,256]{1,0:T(8,128)(2,1)S(1)}, bf16[256,256]{1,0:T(8,128)(2,1)}, u32[]{:S(2)}) %copy-start.1) | copy-done | bytes 131096
  3.1 0.0 copy-start.2
  3.1 0.9 %copy-done.2 = bf16[256,256]{1,0:T(8,128)(2,1)S(1)} copy-done((bf16[256,256]{1,0:T(8,128)(2,1)S(1)}, bf16[256,256]{1,0:T(8,128)(2,1)}, u32[]{:S(2)}) %copy-start.2) | copy-done | bytes 131096
  4.0 0.0 copy-start.3
  4.0 0.9 %copy-done.3 = bf16[256,256]{1,0:T(8,128)(2,1)S(1)} copy-done((bf16[256,256]{1,0:T(8,128)(2,1)S(1)}, bf16[256,256]{1,0:T(8,128)(2,1)}, u32[]{:S(2)}) %copy-start.3) | copy-done | bytes 131096
  4.9 0.0 copy-start.4
  4.9 0.9 %copy-done.4 = bf16[256,256]{1,0:T(8,128)(2,1)S(1)} copy-done((bf16[256,256]{1,0:T(8,128)(2,1)S(1)}, bf16[256,256]{1,0:T(8,128)(2,1)}, u32[]{:S(2)}) %copy-start.4) | copy-done | bytes 131096
  5.8 0.0 copy-start.5
  5.8 0.9 %copy-done.5 = bf16[256,256]{1,0:T(8,128)(2,1)S(1)} copy-done((bf16[256,256]{1,0:T(8,128)(2,1)S(1)}, bf16[256,256]{1,0:T(8,128)(2,1)}, u32[]{:S(2)}) %copy-start.5) | copy-done | bytes 131096
  6.7 0.0 copy-start.6
  6.7 0.9 %copy-done.6 = bf16[256,256]{1,0:T(8,128)(2,1)S(1)} copy-done((bf16[256,256]{1,0:T(8,128)(2,1)S(1)}, bf16[256,256]{1,0:T(8,128)(2,1)}, u32[]{:S(2)}) %copy-start.6) | copy-done | bytes 131096
  7.7 0.0 copy-start.7
  7.7 0.7 copy-done.7
  8.4 0.0 copy-start.8
  8.4 0.7 copy-done.8
  9.1 61.3 %shard_map.161 = (bf16[256,256]{1,0:T(8,128)(2,1)S(1)}, bf16[256,256]{1,0:T(8,128)(2,1)S(1)}, bf16[256,256]{1,0:T(8,128)(2,1)S(1)}, bf16[256,256]{1,0:T(8,128)(2...) custom-call(bf16[256,256]{1,0:T(8,128)(2,1)S(1)} %copy-done, ...), custom_call_target="tpu_custom_call" | custom-call | tf_op jit(solution)/shard_map/pallas_call | solution.py:668
  70.4 0.7 copy.26
  71.0 0.7 copy.27
  71.7 0.7 copy.28
  72.3 0.7 copy.29
  73.0 0.7 copy.30
  73.7 0.6 copy.31
  74.2 0.7 copy.32
  74.9 0.7 copy.33
Async XLA Ops:
  0.6 0.7 copy-start.9
  1.3 0.9 %copy-start = (bf16[256,256]{1,0:T(8,128)(2,1)S(1)}, bf16[256,256]{1,0:T(8,128)(2,1)}, u32[]{:S(2)}) copy-start(bf16[256,256]{1,0:T(8,128)(2,1)} %refs_0_.1) | copy-start | bytes 393220
  2.2 0.9 %copy-start.1 = (bf16[256,256]{1,0:T(8,128)(2,1)S(1)}, bf16[256,256]{1,0:T(8,128)(2,1)}, u32[]{:S(2)}) copy-start(bf16[256,256]{1,0:T(8,128)(2,1)} %refs_1_.1) | copy-start | bytes 393220
  3.1 0.9 %copy-start.2 = (bf16[256,256]{1,0:T(8,128)(2,1)S(1)}, bf16[256,256]{1,0:T(8,128)(2,1)}, u32[]{:S(2)}) copy-start(bf16[256,256]{1,0:T(8,128)(2,1)} %refs_2_.1) | copy-start | bytes 393220
  4.0 0.9 %copy-start.3 = (bf16[256,256]{1,0:T(8,128)(2,1)S(1)}, bf16[256,256]{1,0:T(8,128)(2,1)}, u32[]{:S(2)}) copy-start(bf16[256,256]{1,0:T(8,128)(2,1)} %refs_3_.1) | copy-start | bytes 393220
  4.9 0.9 %copy-start.4 = (bf16[256,256]{1,0:T(8,128)(2,1)S(1)}, bf16[256,256]{1,0:T(8,128)(2,1)}, u32[]{:S(2)}) copy-start(bf16[256,256]{1,0:T(8,128)(2,1)} %refs_7_.1) | copy-start | bytes 393220
  5.8 0.9 %copy-start.5 = (bf16[256,256]{1,0:T(8,128)(2,1)S(1)}, bf16[256,256]{1,0:T(8,128)(2,1)}, u32[]{:S(2)}) copy-start(bf16[256,256]{1,0:T(8,128)(2,1)} %refs_8_.1) | copy-start | bytes 393220
  6.7 0.9 %copy-start.6 = (bf16[256,256]{1,0:T(8,128)(2,1)S(1)}, bf16[256,256]{1,0:T(8,128)(2,1)}, u32[]{:S(2)}) copy-start(bf16[256,256]{1,0:T(8,128)(2,1)} %refs_9_.1) | copy-start | bytes 393220
  7.7 0.7 copy-start.7
  8.4 0.7 copy-start.8

commit v2 on v1

--- a/solution.py
+++ b/solution.py
@@ -11,6 +11,7 @@
 CHUNK = 64
 NX = 4
 FILL = -1e30
+VMEM = 63 * 1024 * 1024
 EPS = 1e-06
 LOG2E = 1.4426950408889634
 NT = (((1,), (1,)), ((), ()))
@@ -66,6 +67,24 @@
 def kernel(
     n_ctx,
     n_tp,
+    gate_h,
+    keyp_h,
+    valp_h,
+    stream_h,
+    decay_h,
+    residue_h,
+    gain_h,
+    query_h,
+    key_h,
+    grad_h,
+    att_h,
+    gateg_h,
+    keypg_h,
+    valpg_h,
+    streamg_h,
+    gaing_h,
+    queryg_h,
+    keyg_h,
     gate,
     keyp,
     valp,
@@ -135,6 +154,8 @@
     ls_r,
     rt_s,
     rt_r,
+    in_s,
+    out_s,
 ):
     b = lax.axis_index("ctx")
     tp = lax.axis_index("tp")
@@ -146,6 +167,38 @@
     across = b + 2 - 4 * y
     scale = HD**-0.5
 
+    loads = [
+        pltpu.make_async_copy(src, dst, in_s.at[i])
+        for i, (src, dst) in enumerate(
+            (
+                (decay_h, decay),
+                (residue_h, residue),
+                (keyp_h, keyp),
+                (valp_h, valp),
+                (query_h, query),
+                (grad_h, grad),
+                (key_h, key),
+                (gate_h, gate),
+                (stream_h, stream),
+                (gain_h, gain),
+            )
+        )
+    ]
+    for load in loads:
+        load.start()
+
+    results = (
+        (att_o, att_h),
+        (gate_o, gateg_h),
+        (keyp_o, keypg_h),
+        (valp_o, valpg_h),
+        (stream_o, streamg_h),
+        (gain_o, gaing_h),
+        (query_o, queryg_h),
+        (key_o, keyg_h),
+    )
+    stores = [pltpu.make_async_copy(v, h, out_s.at[i]) for i, (v, h) in enumerate(results)]
+
     barrier = pltpu.get_barrier_semaphore()
 
     def greet_ctx(r):
@@ -161,6 +214,8 @@
     loop(1, n_ctx, greet_ctx)
     loop(1, n_tp, greet_tp)
 
+    for load in loads[:2]:
+        load.wait()
     chunk_id = lax.broadcasted_iota(jnp.int32, (8, HD), 0) % 4
     chunk_f = chunk_id.astype(F32)
     for m in range(MODES):
@@ -228,6 +283,8 @@
             state_out.at[way], state_in.at[way, src], st_s.at[way, src], st_r.at[way, src], ctx=src
         ).wait_recv()
 
+    for load in loads[2:4]:
+        load.wait()
     mixed = keyp[...].astype(F32) * valp[...].astype(F32)
     xs[0:BLK, :] = mixed[:, :HD]
     xs[BLK:, :] = mixed[:, HD:]
@@ -284,6 +341,8 @@
         sib_copy(t, piece).wait_send()
         targets(t, lambda to: x_copy(t, piece, to).wait_send())
 
+    for load in loads[4:7]:
+        load.wait()
     place(Q, query)
     place(DO, grad)
     place(K, key)
@@ -297,12 +356,13 @@
     pl.semaphore_wait(barrier, n_ctx + n_tp - 2)
 
     loop(b + 1, n_ctx, lambda dst: state_copy(0, dst).start())
-    for t in (Q, DO, K):
+    for t in (Q, K, DO):
         swap_copy(t).start()
-    for t in (Q, DO, K):
+    for t in (Q, K, DO):
         send_piece(t, y)
-    swap_wait(Q)
-    send_piece(Q, 1 - y)
+    for t in (Q, K, DO):
+        swap_wait(t)
+        send_piece(t, 1 - y)
 
     def gather_states(way):
         def hop(i, total):
@@ -327,6 +387,8 @@
             tp_in.at[which], tp_in.at[which], tp_s.at[which], tp_r.at[which], tp=lax.rem(tp + 1, n_tp)
         )
 
+    for load in loads[7:]:
+        load.wait()
     gather_states(0)
     filter_run(False)
     total = stream[...].astype(F32) + gate[...].astype(F32) * jnp.concatenate(
@@ -336,10 +398,6 @@
     tp_out[0] = row_sums(total * total)
     loop(1, n_tp, lambda r: tp_copy(0, r).start())
 
-    for t in (DO, K):
-        swap_wait(t)
-        send_piece(t, 1 - y)
-
     def chip_tile(t, r):
         return big[t, jnp.where(r % 2 == a, x, 4), r // 2]
 
@@ -372,6 +430,24 @@
         piece_wait(K, piece, 4)
     key_scores(x)
 
+    def later_scores(xq):
+        for piece in (0, 1):
+            piece_wait(Q, piece, xq)
+        key_scores(xq)
+
+    loop(x + 1, NX, later_scores)
+
+    def stat_copy(buf, send, recv, to):
+        return remote(buf.at[x], buf.at[x], send.at[to], recv.at[x], ctx=4 * to + mine)
+
+    def stat_wait(buf, send, recv, src):
+        remote(buf.at[src], buf.at[src], send.at[src], recv.at[src], ctx=4 * src + mine).wait_recv()
+
+    def others(body):
+        loop(1, NX, lambda r: body(lax.rem(x + r, NX)))
+
+    others(lambda to: stat_copy(ml, ml_s, ml_r, to).start())
+
     def tp_total(which):
         tp_all(which).wait_recv()
         return jnp.sum(tp_in[which], axis=0) + tp_out[which]
@@ -395,25 +471,6 @@
     swap_copy(V).start()
     send_piece(V, y)
 
-    def later_scores(xq):
-        for piece in (0, 1):
-            piece_wait(Q, piece, xq)
-        key_scores(xq)
-
-    loop(x + 1, NX, later_scores)
-    swap_wait(V)
-    send_piece(V, 1 - y)
-
-    def stat_copy(buf, send, recv, to):
-        return remote(buf.at[x], buf.at[x], send.at[to], recv.at[x], ctx=4 * to + mine)
-
-    def stat_wait(buf, send, recv, src):
-        remote(buf.at[src], buf.at[src], send.at[src], recv.at[src], ctx=4 * src + mine).wait_recv()
-
-    def others(body):
-        loop(1, NX, lambda r: body(lax.rem(x + r, NX)))
-
-    others(lambda to: stat_copy(ml, ml_s, ml_r, to).start())
     others(lambda src: stat_wait(ml, ml_s, ml_r, src))
     tops = jnp.max(ml[:, 0:4, :], axis=0)
     sums = jnp.sum(ml[:, 4:8, :] * jnp.exp2(ml[:, 0:4, :] - tops[None]), axis=0)
@@ -484,6 +541,8 @@
 
     loop(0, 4, value_grads)
 
+    swap_wait(V)
+    send_piece(V, 1 - y)
     for piece in (0, 1):
         piece_wait(V, piece, 4)
     dl[x] = jnp.zeros((8, 2 * BLK), F32)
@@ -518,19 +577,6 @@
     ls[1, 0] = fs[pl.ds(x, 1)]
     sib_stat(1).start()
 
-    dot_col = columns(tp_total(1) / float(n_tp * 2 * HD))
-    inverse2 = jnp.concatenate([inv[...], inv[...]], axis=1)
-    dsummed = inverse2 * (dsum[...] - normed[...] * jnp.concatenate([dot_col, dot_col], axis=1))
-    stream_o[...] = dsummed.astype(BF16)
-    gate_o[...] = (
-        dsummed * jnp.concatenate([conv[0:BLK, :], conv[BLK:, :]], axis=1)
-    ).astype(BF16)
-    back = dsummed * gate[...].astype(F32)
-    xs[0:BLK, :] = back[:, :HD]
-    xs[BLK:, :] = back[:, HD:]
-    filter_ends(True)
-    loop(0, b, lambda dst: state_copy(1, dst).start())
-
     def key_grads(r):
         def add(xq, acc):
             ds = exps[xq, r].astype(F32) * (dprob[xq, r] - fs[pl.ds(xq, 1)])
@@ -539,12 +585,6 @@
         give_back(R_DK, r, lax.fori_loop(x, NX, add, zero_tile))
 
     loop(0, 4, key_grads)
-
-    gather_states(1)
-    filter_run(True)
-    dmixed = jnp.concatenate([conv[0:BLK, :], conv[BLK:, :]], axis=1)
-    keyp_o[...] = (dmixed * valp[...].astype(F32)).astype(BF16)
-    valp_o[...] = (dmixed * keyp[...].astype(F32)).astype(BF16)
 
     for kind in (0, 1):
         sib_stat(kind).wait_recv()
@@ -585,11 +625,39 @@
 
     loop(0, 4, query_rows)
 
+    dot_col = columns(tp_total(1) / float(n_tp * 2 * HD))
+    inverse2 = jnp.concatenate([inv[...], inv[...]], axis=1)
+    dsummed = inverse2 * (dsum[...] - normed[...] * jnp.concatenate([dot_col, dot_col], axis=1))
+    stream_o[...] = dsummed.astype(BF16)
+    gate_o[...] = (
+        dsummed * jnp.concatenate([conv[0:BLK, :], conv[BLK:, :]], axis=1)
+    ).astype(BF16)
+    stores[4].start()
+    stores[1].start()
+    back = dsummed * gate[...].astype(F32)
+    xs[0:BLK, :] = back[:, :HD]
+    xs[BLK:, :] = back[:, HD:]
+    filter_ends(True)
+    loop(0, b, lambda dst: state_copy(1, dst).start())
+
     remote(gain_in, gain_in, ga_s.at[0], ga_r.at[0], ctx=sibling).wait_recv()
     gain_o[...] = jnp.sum(gain_in[...], axis=0) + gain_out[...]
+    stores[5].start()
     key_o[...] = take_back(R_DK).astype(BF16)
+    stores[7].start()
     att_o[...] = take_back(R_ATT).astype(BF16)
+    stores[0].start()
     query_o[...] = take_back(R_DQ).astype(BF16)
+    stores[6].start()
+
+    gather_states(1)
+    filter_run(True)
+    dmixed = jnp.concatenate([conv[0:BLK, :], conv[BLK:, :]], axis=1)
+    keyp_o[...] = (dmixed * valp[...].astype(F32)).astype(BF16)
+    valp_o[...] = (dmixed * keyp[...].astype(F32)).astype(BF16)
+
+    stores[2].start()
+    stores[3].start()
 
     loop(b + 1, n_ctx, lambda dst: state_copy(0, dst).wait_send())
     loop(0, b, lambda dst: state_copy(1, dst).wait_send())
@@ -605,12 +673,26 @@
     others(lambda to: stat_copy(dl, dl_s, dl_r, to).wait_send())
     for t in (R_DV, R_DK, R_ATT, R_DQ):
         quad(lambda r: ret_copy(t, r).wait_send())
+    for copy in stores:
+        copy.wait()
+
+
+def store(*refs):
+    held, sem = refs[16:24], refs[24]
+    arrive = [pltpu.make_async_copy(refs[i], held[i], sem.at[0, i]) for i in range(8)]
+    leave = [pltpu.make_async_copy(held[i], refs[8 + i], sem.at[1, i]) for i in range(8)]
+    for copy in arrive:
+        copy.start()
+    for one, other in zip(arrive, leave):
+        one.wait()
+        other.start()
+    for copy in leave:
+        copy.wait()
 
 
 def on_device(n_ctx, n_tp, *arrays):
     (gate, keyp, valp, stream, decay, residue, gain, query, key, grad) = arrays
     rows, chans = stream.shape
-    vmem = pl.BlockSpec(memory_space=pltpu.VMEM)
     full = jax.ShapeDtypeStruct((rows, chans), BF16)
     dma = pltpu.SemaphoreType.DMA
 
@@ -618,6 +700,13 @@
         kernel(n_ctx, n_tp, *refs)
 
     scratch = [
+        *[pltpu.VMEM((rows, chans), BF16)] * 4,
+        *[pltpu.VMEM((MODES, chans), F32)] * 2,
+        pltpu.VMEM((1, chans), F32),
+        *[pltpu.VMEM((rows, chans), BF16)] * 3,
+        *[pltpu.VMEM((rows, chans), BF16)] * 5,
+        pltpu.VMEM((1, chans), F32),
+        *[pltpu.VMEM((rows, chans), BF16)] * 2,
         pltpu.VMEM((2 * BLK, HD), F32),
         pltpu.VMEM((2 * BLK, HD), F32),
         *[pltpu.VMEM((MODES, 8, HD), F32)] * 6,
@@ -664,17 +753,29 @@
         dma((2,)),
         dma((4, 4)),
         dma((4, 4)),
+        dma((10,)),
+        dma((8,)),
     ]
+    hbm = pl.BlockSpec(memory_space=pltpu.HBM)
+    shapes = (full,) * 5 + (jax.ShapeDtypeStruct((1, chans), F32),) + (full,) * 2
     outs = pl.pallas_call(
         body,
-        out_shape=(full,) * 5 + (jax.ShapeDtypeStruct((1, chans), F32),) + (full,) * 2,
-        in_specs=[vmem] * 10,
-        out_specs=(vmem,) * 8,
+        out_shape=shapes,
+        in_specs=[hbm] * 10,
+        out_specs=(hbm,) * 8,
         scratch_shapes=scratch,
         compiler_params=pltpu.CompilerParams(
-            collective_id=0, has_side_effects=True, vmem_limit_bytes=48 * 1024 * 1024
+            collective_id=0, has_side_effects=True, vmem_limit_bytes=VMEM
         ),
     )(gate, keyp, valp, stream, decay, residue, gain.reshape(1, chans), query, key, grad)
+    outs = pl.pallas_call(
+        store,
+        out_shape=shapes,
+        in_specs=[hbm] * 8,
+        out_specs=(hbm,) * 8,
+        scratch_shapes=[*[pltpu.VMEM(s.shape, s.dtype) for s in shapes], dma((2, 8))],
+        compiler_params=pltpu.CompilerParams(vmem_limit_bytes=VMEM),
+    )(*outs)
     return outs[:5] + (outs[5].reshape(chans),) + outs[6:]
 
 

time: 76 us -> 61.1 us (0.80)
  local copies, waits for them, and re-layouts: 13.6 us -> 0 us
  Pallas kernels: 61.3 us -> 60.2 us
    unnamed x28 -> x0, local copies, waits for them, and re-layouts: 13.6 us -> none
    pallas_call x1 -> x2, Pallas kernels: 61.3 us -> 60.2 us  [the longest x1 58.2 us: on_device(): pl.pallas_call(body, out_shape=shapes, in_specs=[hbm] * 10, out_specs=(hb...]
where the time goes in v2:
time: 61.1 us; the launch traced here: 60.9 us
  Pallas kernels  60.2 us (99%)
  between operations  0.64 us (1%)
    pallas_call x1, Pallas kernels, on_device(): pl.pallas_call(body, out_shape=shapes, in_specs=[hbm] * 10, out_specs=(hb...  58.2 us
    pallas_call x1, Pallas kernels, on_device(): pl.pallas_call(store, out_shape=shapes, in_specs=[hbm] * 8, out_specs=(hb...  2.05 us

profile of v2, /device:TPU:1, one launch (start us, length us, event | category | flops | bytes accessed | tf_op | source)
XLA Modules:
  0.0 60.9 jit_solution(2589337140765748627)
XLA Ops:
  0.6 58.2 %shard_map.161 = (bf16[256,256]{1,0:T(8,128)(2,1)}, bf16[256,256]{1,0:T(8,128)(2,1)}, bf16[256,256]{1,0:T(8,128)(2,1)}, bf16[256,256]{1,0:T(8,128)(2,1)}, bf16[2...) custom-call(bf16[256,256]{1,0:T(8,128)(2,1)} %refs_0_.1, ...), custom_call_target="tpu_custom_call" | custom-call | tf_op jit(solution)/shard_map/pallas_call | solution.py:761
  58.8 2.1 %shard_map.162 = (bf16[256,256]{1,0:T(8,128)(2,1)}, bf16[256,256]{1,0:T(8,128)(2,1)}, bf16[256,256]{1,0:T(8,128)(2,1)}, bf16[256,256]{1,0:T(8,128)(2,1)}, bf16[2...) custom-call(bf16[256,256]{1,0:T(8,128)(2,1)} %get-tuple-element.24.refs_0_, ...), custom_call_target="tpu_custom_call" | custom-call | tf_op jit(solution)/shard_map/pallas_call | solution.py:771

commit v3 on v2

--- a/solution.py
+++ b/solution.py
@@ -130,7 +130,7 @@
     ml,
     dl,
     fs,
-    dos,
+    acc,
     qs,
     ls,
     lcol,
@@ -333,9 +333,12 @@
         else:
             loop(x + 1, NX, body)
 
+    def send_x(t, piece):
+        targets(t, lambda to: x_copy(t, piece, to).start())
+
     def send_piece(t, piece):
         sib_copy(t, piece).start()
-        targets(t, lambda to: x_copy(t, piece, to).start())
+        send_x(t, piece)
 
     def drain_piece(t, piece):
         sib_copy(t, piece).wait_send()
@@ -358,11 +361,17 @@
     loop(b + 1, n_ctx, lambda dst: state_copy(0, dst).start())
     for t in (Q, K, DO):
         swap_copy(t).start()
-    for t in (Q, K, DO):
-        send_piece(t, y)
-    for t in (Q, K, DO):
-        swap_wait(t)
-        send_piece(t, 1 - y)
+    send_x(Q, y)
+    sib_copy(K, y).start()
+    swap_wait(Q)
+    send_x(Q, 1 - y)
+    swap_wait(K)
+    sib_copy(K, 1 - y).start()
+    send_piece(DO, y)
+    swap_wait(DO)
+    send_piece(DO, 1 - y)
+    for piece in (0, 1):
+        sib_copy(Q, piece).start()
 
     def gather_states(way):
         def hop(i, total):
@@ -397,6 +406,8 @@
     normed[...] = total
     tp_out[0] = row_sums(total * total)
     loop(1, n_tp, lambda r: tp_copy(0, r).start())
+    for piece in (0, 1):
+        send_x(K, piece)
 
     def chip_tile(t, r):
         return big[t, jnp.where(r % 2 == a, x, 4), r // 2]
@@ -408,32 +419,31 @@
     ml[x, 0:4] = neg
     ml[x, 4:8] = jnp.zeros_like(neg)
 
-    def key_scores(xq):
-        def tile(r, top):
-            s = dot_nt(chip_tile(K, r), x_tile(Q, xq)) * (scale * LOG2E)
-            s = jnp.where(rel[...] >= BLK * r - 4 * BLK * (xq - x), s, FILL)
+    def key_scores(xq, own):
+        queries = x_tile(Q, xq)
+        top = jnp.full((1, 2 * BLK), FILL, F32)
+        for r in range(4):
+            s = dot_nt(chip_tile(K, r), queries) * (scale * LOG2E)
+            if own:
+                s = jnp.where(rel[...] >= BLK * r, s, FILL)
             work[r] = s
-            return jnp.maximum(top, jnp.max(s, axis=0, keepdims=True))
-
-        top = lax.fori_loop(0, 4, tile, jnp.full((1, 2 * BLK), FILL, F32))
-
-        def tile_exp(r, total):
+            top = jnp.maximum(top, jnp.max(s, axis=0, keepdims=True))
+        total = jnp.zeros((1, 2 * BLK), F32)
+        for r in range(4):
             e = jnp.exp2(work[r] - top)
             exps[xq, r] = e.astype(BF16)
-            return total + jnp.sum(e, axis=0, keepdims=True)
-
-        total = lax.fori_loop(0, 4, tile_exp, jnp.zeros((1, 2 * BLK), F32))
+            total = total + jnp.sum(e, axis=0, keepdims=True)
         ml[x, pl.ds(xq, 1)] = top
         ml[x, pl.ds(4 + xq, 1)] = total
 
     for piece in (0, 1):
         piece_wait(K, piece, 4)
-    key_scores(x)
+    key_scores(x, True)
 
     def later_scores(xq):
         for piece in (0, 1):
             piece_wait(Q, piece, xq)
-        key_scores(xq)
+        key_scores(xq, False)
 
     loop(x + 1, NX, later_scores)
 
@@ -484,18 +494,20 @@
     ls[0, 0] = fs[pl.ds(4 + x, 1)]
     sib_stat(0).start()
 
-    def scale_rows(xq):
+    def value_grads(xq, first):
         f = columns(fs[pl.ds(xq, 1)])
-        dos[xq] = (x_tile(DO, xq).astype(F32) * f).astype(BF16)
-        qs[xq] = (x_tile(Q, xq).astype(F32) * (f * scale)).astype(BF16)
-
-    def later_rows(xq):
+        cotangents = (x_tile(DO, xq).astype(F32) * f).astype(BF16)
+        for r in range(4):
+            part = dot(exps[xq, r], cotangents)
+            acc[0, r] = part if first else acc[0, r] + part
+
+    def later_value_grads(xq):
         for piece in (0, 1):
             piece_wait(DO, piece, xq)
-        scale_rows(xq)
-
-    scale_rows(x)
-    loop(x + 1, NX, later_rows)
+        value_grads(xq, False)
+
+    value_grads(x, True)
+    loop(x + 1, NX, later_value_grads)
 
     def ret_copy(t, r):
         return remote(
@@ -531,15 +543,8 @@
             axis=1,
         )
 
-    zero_tile = jnp.zeros((BLK, HD), F32)
-
-    def value_grads(r):
-        total = lax.fori_loop(
-            x, NX, lambda xq, acc: acc + dot(exps[xq, r], dos[xq]), zero_tile
-        )
-        give_back(R_DV, r, total)
-
-    loop(0, 4, value_grads)
+    for r in range(4):
+        give_back(R_DV, r, acc[0, r])
 
     swap_wait(V)
     send_piece(V, 1 - y)
@@ -548,13 +553,15 @@
     dl[x] = jnp.zeros((8, 2 * BLK), F32)
 
     def key_delta(xq):
-        def tile(r, total):
-            dp = dot_nt(chip_tile(V, r), x_tile(DO, xq))
+        f = fs[pl.ds(xq, 1)]
+        qs[xq] = (x_tile(Q, xq).astype(F32) * (columns(f) * scale)).astype(BF16)
+        cotangents = x_tile(DO, xq)
+        total = jnp.zeros((1, 2 * BLK), F32)
+        for r in range(4):
+            dp = dot_nt(chip_tile(V, r), cotangents)
             dprob[xq, r] = dp
-            return total + jnp.sum(exps[xq, r].astype(F32) * dp, axis=0, keepdims=True)
-
-        total = lax.fori_loop(0, 4, tile, jnp.zeros((1, 2 * BLK), F32))
-        dl[x, pl.ds(xq, 1)] = total * fs[pl.ds(xq, 1)]
+            total = total + jnp.sum(exps[xq, r].astype(F32) * dp, axis=0, keepdims=True)
+        dl[x, pl.ds(xq, 1)] = total * f
 
     loop(x, NX, key_delta)
     others(lambda to: stat_copy(dl, dl_s, dl_r, to).start())
@@ -577,14 +584,17 @@
     ls[1, 0] = fs[pl.ds(x, 1)]
     sib_stat(1).start()
 
-    def key_grads(r):
-        def add(xq, acc):
-            ds = exps[xq, r].astype(F32) * (dprob[xq, r] - fs[pl.ds(xq, 1)])
-            return acc + dot(ds.astype(BF16), qs[xq])
-
-        give_back(R_DK, r, lax.fori_loop(x, NX, add, zero_tile))
-
-    loop(0, 4, key_grads)
+    def key_grads(xq, first):
+        delta = fs[pl.ds(xq, 1)]
+        for r in range(4):
+            ds = exps[xq, r].astype(F32) * (dprob[xq, r] - delta)
+            part = dot(ds.astype(BF16), qs[xq])
+            acc[0, r] = part if first else acc[0, r] + part
+
+    key_grads(x, True)
+    loop(x + 1, NX, lambda xq: key_grads(xq, False))
+    for r in range(4):
+        give_back(R_DK, r, acc[0, r])
 
     for kind in (0, 1):
         sib_stat(kind).wait_recv()
@@ -604,26 +614,27 @@
     def wide(col):
         return jnp.concatenate([col] * 4, axis=1)
 
-    def query_rows(r):
-        who = jnp.where(r % 2 == a, 0, 1)
-
-        def add(xk, acc):
-            att, dq = acc
-            s = dot_nt(chip_tile(Q, r), x_tile(K, xk)) * (scale * LOG2E)
+    def query_rows(xk, own):
+        keys = x_tile(K, xk)
+        vals = x_tile(V, xk)
+        for r in range(4):
+            who = jnp.where(r % 2 == a, 0, 1)
+            s = dot_nt(chip_tile(Q, r), keys) * (scale * LOG2E)
             p = jnp.exp2(s - wide(lcol[0, who, r // 2]))
-            p = jnp.where(rel[...] <= BLK * r + 4 * BLK * (x - xk), p, 0.0)
-            dp = dot_nt(chip_tile(DO, r), x_tile(V, xk))
+            if own:
+                p = jnp.where(rel[...] <= BLK * r, p, 0.0)
+            dp = dot_nt(chip_tile(DO, r), vals)
             ds = p * (dp - wide(lcol[1, who, r // 2]))
-            return (
-                att + dot(p.astype(BF16), x_tile(V, xk)),
-                dq + dot(ds.astype(BF16), x_tile(K, xk)),
-            )
-
-        att, dq = lax.fori_loop(0, x + 1, add, (zero_tile, zero_tile))
-        give_back(R_ATT, r, att)
-        give_back(R_DQ, r, dq * scale)
-
-    loop(0, 4, query_rows)
+            att = dot(p.astype(BF16), vals)
+            dq = dot(ds.astype(BF16), keys)
+            acc[0, r] = att if own else acc[0, r] + att
+            acc[1, r] = dq if own else acc[1, r] + dq
+
+    query_rows(x, True)
+    loop(0, x, lambda xk: query_rows(xk, False))
+    for r in range(4):
+        give_back(R_ATT, r, acc[0, r])
+        give_back(R_DQ, r, acc[1, r] * scale)
 
     dot_col = columns(tp_total(1) / float(n_tp * 2 * HD))
     inverse2 = jnp.concatenate([inv[...], inv[...]], axis=1)
@@ -729,7 +740,7 @@
         pltpu.VMEM((NX, 8, 2 * BLK), F32),
         pltpu.VMEM((NX, 8, 2 * BLK), F32),
         pltpu.VMEM((8, 2 * BLK), F32),
-        pltpu.VMEM((NX, 2 * BLK, HD), BF16),
+        pltpu.VMEM((2, 4, BLK, HD), F32),
         pltpu.VMEM((NX, 2 * BLK, HD), BF16),
         pltpu.VMEM((2, 2, 1, 2 * BLK), F32),
         pltpu.VMEM((2, 2, 2, BLK, HD), F32),

time: 61.1 us -> 56.3 us (0.921)
  Pallas kernels: 60.2 us -> 55.5 us
    pallas_call x1, Pallas kernels: 58.2 us -> 53.5 us  [on_device(): pl.pallas_call(body, out_shape=shapes, in_specs=[hbm] * 10, out_specs=(hb...]
where the time goes in v3:
time: 56.3 us; the launch traced here: 56.2 us
  Pallas kernels  55.5 us (99%)
  between operations  0.64 us (1%)
    pallas_call x1, Pallas kernels, on_device(): pl.pallas_call(body, out_shape=shapes, in_specs=[hbm] * 10, out_specs=(hb...  53.5 us
    pallas_call x1, Pallas kernels, on_device(): pl.pallas_call(store, out_shape=shapes, in_specs=[hbm] * 8, out_specs=(hb...  2.05 us

profile of v3, /device:TPU:1, one launch (start us, length us, event | category | flops | bytes accessed | tf_op | source)
XLA Modules:
  0.0 56.2 jit_solution(7497681955189369130)
XLA Ops:
  0.6 53.5 %shard_map.161 = (bf16[256,256]{1,0:T(8,128)(2,1)}, bf16[256,256]{1,0:T(8,128)(2,1)}, bf16[256,256]{1,0:T(8,128)(2,1)}, bf16[256,256]{1,0:T(8,128)(2,1)}, bf16[2...) custom-call(bf16[256,256]{1,0:T(8,128)(2,1)} %refs_0_.1, ...), custom_call_target="tpu_custom_call" | custom-call | tf_op jit(solution)/shard_map/pallas_call | solution.py:772
  54.1 2.1 %shard_map.162 = (bf16[256,256]{1,0:T(8,128)(2,1)}, bf16[256,256]{1,0:T(8,128)(2,1)}, bf16[256,256]{1,0:T(8,128)(2,1)}, bf16[256,256]{1,0:T(8,128)(2,1)}, bf16[2...) custom-call(bf16[256,256]{1,0:T(8,128)(2,1)} %get-tuple-element.24.refs_0_, ...), custom_call_target="tpu_custom_call" | custom-call | tf_op jit(solution)/shard_map/pallas_call | solution.py:782

commit v4 on v3

--- a/solution.py
+++ b/solution.py
@@ -124,6 +124,7 @@
     swap,
     big,
     exps,
+    probs,
     work,
     dprob,
     rel,
@@ -211,8 +212,11 @@
             barrier, 1, device_id={"tp": lax.rem(tp + r, n_tp)}, device_id_type=pl.DeviceIdType.MESH
         )
 
-    loop(1, n_ctx, greet_ctx)
-    loop(1, n_tp, greet_tp)
+    half = n_tp // 2
+    for r in sorted(range(1, n_tp), key=lambda r: -min(r % half, half - r % half)):
+        greet_tp(r)
+    for r in range(1, n_ctx):
+        greet_ctx(r)
 
     for load in loads[:2]:
         load.wait()
@@ -358,11 +362,12 @@
 
     pl.semaphore_wait(barrier, n_ctx + n_tp - 2)
 
-    loop(b + 1, n_ctx, lambda dst: state_copy(0, dst).start())
-    for t in (Q, K, DO):
-        swap_copy(t).start()
+    swap_copy(Q).start()
+    swap_copy(K).start()
     send_x(Q, y)
     sib_copy(K, y).start()
+    loop(b + 1, n_ctx, lambda dst: state_copy(0, dst).start())
+    swap_copy(DO).start()
     swap_wait(Q)
     send_x(Q, 1 - y)
     swap_wait(K)
@@ -566,6 +571,45 @@
     loop(x, NX, key_delta)
     others(lambda to: stat_copy(dl, dl_s, dl_r, to).start())
 
+    def wide(col):
+        return jnp.concatenate([col] * 4, axis=1)
+
+    def side(r):
+        return jnp.where(r % 2 == a, 0, 1)
+
+    sib_stat(0).wait_recv()
+    for who in (0, 1):
+        lcol[0, who] = columns(ls[0, who]).reshape(2, BLK, HD)
+    for piece in (0, 1):
+        piece_wait(Q, piece, 4)
+
+    def query_probs(xk, own):
+        keys = x_tile(K, xk)
+        for r in range(4):
+            s = dot_nt(chip_tile(Q, r), keys) * (scale * LOG2E)
+            p = jnp.exp2(s - wide(lcol[0, side(r), r // 2]))
+            if own:
+                p = jnp.where(rel[...] <= BLK * r, p, 0.0)
+            probs[xk, r] = p.astype(BF16)
+
+    def earlier_probs(xk):
+        for piece in (0, 1):
+            piece_wait(K, piece, xk)
+        query_probs(xk, False)
+
+    query_probs(x, True)
+    loop(0, x, earlier_probs)
+
+    loop(b + 1, n_ctx, lambda dst: state_copy(0, dst).wait_send())
+    for t in (Q, DO, K, V):
+        swap_copy(t).wait_send()
+    for t in (Q, DO, K):
+        for piece in (0, 1):
+            drain_piece(t, piece)
+    tp_all(0).wait_send()
+    sib_stat(0).wait_send()
+    others(lambda to: stat_copy(ml, ml_s, ml_r, to).wait_send())
+
     dvalues = take_back(R_DV)
     dsum[...] = dvalues * gain[...]
     tp_out[1] = row_sums(dsum[...] * normed[...])
@@ -591,65 +635,79 @@
             part = dot(ds.astype(BF16), qs[xq])
             acc[0, r] = part if first else acc[0, r] + part
 
-    key_grads(x, True)
-    loop(x + 1, NX, lambda xq: key_grads(xq, False))
-    for r in range(4):
-        give_back(R_DK, r, acc[0, r])
-
-    for kind in (0, 1):
-        sib_stat(kind).wait_recv()
-        for who in (0, 1):
-            lcol[kind, who] = columns(ls[kind, who]).reshape(2, BLK, HD)
-    for t in (Q, DO):
-        for piece in (0, 1):
-            piece_wait(t, piece, 4)
-
-    def earlier_wait(src):
-        for t in (K, V):
-            for piece in (0, 1):
-                piece_wait(t, piece, src)
-
-    loop(0, x, earlier_wait)
-
-    def wide(col):
-        return jnp.concatenate([col] * 4, axis=1)
+    sib_stat(1).wait_recv()
+    for who in (0, 1):
+        lcol[1, who] = columns(ls[1, who]).reshape(2, BLK, HD)
+    for piece in (0, 1):
+        piece_wait(DO, piece, 4)
 
     def query_rows(xk, own):
         keys = x_tile(K, xk)
         vals = x_tile(V, xk)
         for r in range(4):
-            who = jnp.where(r % 2 == a, 0, 1)
-            s = dot_nt(chip_tile(Q, r), keys) * (scale * LOG2E)
-            p = jnp.exp2(s - wide(lcol[0, who, r // 2]))
-            if own:
-                p = jnp.where(rel[...] <= BLK * r, p, 0.0)
+            p = probs[xk, r]
             dp = dot_nt(chip_tile(DO, r), vals)
-            ds = p * (dp - wide(lcol[1, who, r // 2]))
-            att = dot(p.astype(BF16), vals)
+            ds = p.astype(F32) * (dp - wide(lcol[1, side(r), r // 2]))
+            att = dot(p, vals)
             dq = dot(ds.astype(BF16), keys)
             acc[0, r] = att if own else acc[0, r] + att
             acc[1, r] = dq if own else acc[1, r] + dq
 
-    query_rows(x, True)
-    loop(0, x, lambda xk: query_rows(xk, False))
-    for r in range(4):
-        give_back(R_ATT, r, acc[0, r])
-        give_back(R_DQ, r, acc[1, r] * scale)
+    def earlier_rows(xk):
+        for piece in (0, 1):
+            piece_wait(V, piece, xk)
+        query_rows(xk, False)
+
+    def all_key_grads():
+        key_grads(x, True)
+        loop(x + 1, NX, lambda xq: key_grads(xq, False))
+        for r in range(4):
+            give_back(R_DK, r, acc[0, r])
+
+    def all_query_rows():
+        query_rows(x, True)
+        loop(0, x, earlier_rows)
+        for r in range(4):
+            give_back(R_ATT, r, acc[0, r])
+            give_back(R_DQ, r, acc[1, r] * scale)
+
+    pl.when(x < NX // 2)(all_key_grads)
+    pl.when(x >= NX // 2)(all_query_rows)
 
     dot_col = columns(tp_total(1) / float(n_tp * 2 * HD))
     inverse2 = jnp.concatenate([inv[...], inv[...]], axis=1)
     dsummed = inverse2 * (dsum[...] - normed[...] * jnp.concatenate([dot_col, dot_col], axis=1))
+    back = dsummed * gate[...].astype(F32)
+    xs[0:BLK, :] = back[:, :HD]
+    xs[BLK:, :] = back[:, HD:]
+    filter_ends(True)
+    loop(0, b, lambda dst: state_copy(1, dst).start())
     stream_o[...] = dsummed.astype(BF16)
     gate_o[...] = (
         dsummed * jnp.concatenate([conv[0:BLK, :], conv[BLK:, :]], axis=1)
     ).astype(BF16)
     stores[4].start()
     stores[1].start()
-    back = dsummed * gate[...].astype(F32)
-    xs[0:BLK, :] = back[:, :HD]
-    xs[BLK:, :] = back[:, HD:]
-    filter_ends(True)
-    loop(0, b, lambda dst: state_copy(1, dst).start())
+
+    pl.when(x < NX // 2)(all_query_rows)
+    pl.when(x >= NX // 2)(all_key_grads)
+
+    for piece in (0, 1):
+        drain_piece(V, piece)
+    tp_all(1).wait_send()
+    sib_stat(1).wait_send()
+    remote(gain_in, gain_in, ga_s.at[0], ga_r.at[0], ctx=sibling).wait_send()
+    others(lambda to: stat_copy(dl, dl_s, dl_r, to).wait_send())
+    quad(lambda r: ret_copy(R_DV, r).wait_send())
+
+    gather_states(1)
+    filter_run(True)
+    dmixed = jnp.concatenate([conv[0:BLK, :], conv[BLK:, :]], axis=1)
+    keyp_o[...] = (dmixed * valp[...].astype(F32)).astype(BF16)
+    valp_o[...] = (dmixed * keyp[...].astype(F32)).astype(BF16)
+
+    stores[2].start()
+    stores[3].start()
 
     remote(gain_in, gain_in, ga_s.at[0], ga_r.at[0], ctx=sibling).wait_recv()
     gain_o[...] = jnp.sum(gain_in[...], axis=0) + gain_out[...]
@@ -661,28 +719,8 @@
     query_o[...] = take_back(R_DQ).astype(BF16)
     stores[6].start()
 
-    gather_states(1)
-    filter_run(True)
-    dmixed = jnp.concatenate([conv[0:BLK, :], conv[BLK:, :]], axis=1)
-    keyp_o[...] = (dmixed * valp[...].astype(F32)).astype(BF16)
-    valp_o[...] = (dmixed * keyp[...].astype(F32)).astype(BF16)
-
-    stores[2].start()
-    stores[3].start()
-
-    loop(b + 1, n_ctx, lambda dst: state_copy(0, dst).wait_send())
     loop(0, b, lambda dst: state_copy(1, dst).wait_send())
-    for t in (Q, DO, K, V):
-        swap_copy(t).wait_send()
-        for piece in (0, 1):
-            drain_piece(t, piece)
-    for which in (0, 1):
-        tp_all(which).wait_send()
-        sib_stat(which).wait_send()
-    remote(gain_in, gain_in, ga_s.at[0], ga_r.at[0], ctx=sibling).wait_send()
-    others(lambda to: stat_copy(ml, ml_s, ml_r, to).wait_send())
-    others(lambda to: stat_copy(dl, dl_s, dl_r, to).wait_send())
-    for t in (R_DV, R_DK, R_ATT, R_DQ):
+    for t in (R_DK, R_ATT, R_DQ):
         quad(lambda r: ret_copy(t, r).wait_send())
     for copy in stores:
         copy.wait()
@@ -733,6 +771,7 @@
         pltpu.VMEM((BLK, 2 * HD), F32),
         pltpu.VMEM((4, BLK, HD), BF16),
         pltpu.VMEM((4, 5, 2, BLK, HD), BF16),
+        pltpu.VMEM((NX, 4, BLK, 2 * BLK), BF16),
         pltpu.VMEM((NX, 4, BLK, 2 * BLK), BF16),
         pltpu.VMEM((4, BLK, 2 * BLK), F32),
         pltpu.VMEM((NX, 4, BLK, 2 * BLK), F32),

time: 56.3 us -> 55 us (0.977)
  Pallas kernels: 55.5 us -> 54.2 us
    pallas_call x1, Pallas kernels: 53.5 us -> 52.2 us  [on_device(): pl.pallas_call(body, out_shape=shapes, in_specs=[hbm] * 10, out_specs=(hb...]
where the time goes in v4:
time: 55 us; the launch traced here: 54.9 us
  Pallas kernels  54.2 us (99%)
  between operations  0.64 us (1%)
    pallas_call x1, Pallas kernels, on_device(): pl.pallas_call(body, out_shape=shapes, in_specs=[hbm] * 10, out_specs=(hb...  52.2 us
    pallas_call x1, Pallas kernels, on_device(): pl.pallas_call(store, out_shape=shapes, in_specs=[hbm] * 8, out_specs=(hb...  2.05 us

profile of v4, /device:TPU:1, one launch (start us, length us, event | category | flops | bytes accessed | tf_op | source)
XLA Modules:
  0.0 54.9 jit_solution(14358124621021366461)
XLA Ops:
  0.6 52.2 %shard_map.161 = (bf16[256,256]{1,0:T(8,128)(2,1)}, bf16[256,256]{1,0:T(8,128)(2,1)}, bf16[256,256]{1,0:T(8,128)(2,1)}, bf16[256,256]{1,0:T(8,128)(2,1)}, bf16[2...) custom-call(bf16[256,256]{1,0:T(8,128)(2,1)} %refs_0_.1, ...), custom_call_target="tpu_custom_call" | custom-call | tf_op jit(solution)/shard_map/pallas_call | solution.py:811
  52.8 2.1 %shard_map.162 = (bf16[256,256]{1,0:T(8,128)(2,1)}, bf16[256,256]{1,0:T(8,128)(2,1)}, bf16[256,256]{1,0:T(8,128)(2,1)}, bf16[256,256]{1,0:T(8,128)(2,1)}, bf16[2...) custom-call(bf16[256,256]{1,0:T(8,128)(2,1)} %get-tuple-element.24.refs_0_, ...), custom_call_target="tpu_custom_call" | custom-call | tf_op jit(solution)/shard_map/pallas_call | solution.py:821

commit v5 on v4

--- a/solution.py
+++ b/solution.py
@@ -131,6 +131,7 @@
     ml,
     dl,
     fs,
+    dos,
     acc,
     qs,
     ls,
@@ -484,6 +485,13 @@
         swap[V] = vals[:, :HD]
 
     swap_copy(V).start()
+    remote(
+        swap.at[V],
+        big.at[V, 4, y],
+        bg_s.at[V, 1 - y, x],
+        bg_r.at[V, y, 4],
+        ctx=across + 1 - 2 * a,
+    ).start()
     send_piece(V, y)
 
     others(lambda src: stat_wait(ml, ml_s, ml_r, src))
@@ -499,20 +507,17 @@
     ls[0, 0] = fs[pl.ds(4 + x, 1)]
     sib_stat(0).start()
 
-    def value_grads(xq, first):
+    def scale_rows(xq):
         f = columns(fs[pl.ds(xq, 1)])
-        cotangents = (x_tile(DO, xq).astype(F32) * f).astype(BF16)
-        for r in range(4):
-            part = dot(exps[xq, r], cotangents)
-            acc[0, r] = part if first else acc[0, r] + part
-
-    def later_value_grads(xq):
+        dos[xq] = (x_tile(DO, xq).astype(F32) * f).astype(BF16)
+
+    def later_rows(xq):
         for piece in (0, 1):
             piece_wait(DO, piece, xq)
-        value_grads(xq, False)
-
-    value_grads(x, True)
-    loop(x + 1, NX, later_value_grads)
+        scale_rows(xq)
+
+    scale_rows(x)
+    loop(x + 1, NX, later_rows)
 
     def ret_copy(t, r):
         return remote(
@@ -548,11 +553,20 @@
             axis=1,
         )
 
-    for r in range(4):
-        give_back(R_DV, r, acc[0, r])
+    for row in (1 - y, y):
+
+        def value_grads(xq):
+            for r in (2 * row, 2 * row + 1):
+                acc[0, r] = acc[0, r] + dot(exps[xq, r], dos[xq])
+
+        for r in (2 * row, 2 * row + 1):
+            acc[0, r] = dot(exps[x, r], dos[x])
+        loop(x + 1, NX, value_grads)
+        for r in (2 * row, 2 * row + 1):
+            give_back(R_DV, r, acc[0, r])
 
     swap_wait(V)
-    send_piece(V, 1 - y)
+    send_x(V, 1 - y)
     for piece in (0, 1):
         piece_wait(V, piece, 4)
     dl[x] = jnp.zeros((8, 2 * BLK), F32)
@@ -671,8 +685,7 @@
             give_back(R_ATT, r, acc[0, r])
             give_back(R_DQ, r, acc[1, r] * scale)
 
-    pl.when(x < NX // 2)(all_key_grads)
-    pl.when(x >= NX // 2)(all_query_rows)
+    all_query_rows()
 
     dot_col = columns(tp_total(1) / float(n_tp * 2 * HD))
     inverse2 = jnp.concatenate([inv[...], inv[...]], axis=1)
@@ -689,8 +702,7 @@
     stores[4].start()
     stores[1].start()
 
-    pl.when(x < NX // 2)(all_query_rows)
-    pl.when(x >= NX // 2)(all_key_grads)
+    all_key_grads()
 
     for piece in (0, 1):
         drain_piece(V, piece)
@@ -779,6 +791,7 @@
         pltpu.VMEM((NX, 8, 2 * BLK), F32),
         pltpu.VMEM((NX, 8, 2 * BLK), F32),
         pltpu.VMEM((8, 2 * BLK), F32),
+        pltpu.VMEM((NX, 2 * BLK, HD), BF16),
         pltpu.VMEM((2, 4, BLK, HD), F32),
         pltpu.VMEM((NX, 2 * BLK, HD), BF16),
         pltpu.VMEM((2, 2, 1, 2 * BLK), F32),

time: 55 us -> 55.1 us (level)
  no operation moved by 1% of the time
where the time goes in v5:
time: 55.1 us; the launch traced here: 54.6 us
  Pallas kernels  53.9 us (98%)
  between operations  0.64 us (1%)
    pallas_call x1, Pallas kernels, on_device(): pl.pallas_call(body, out_shape=shapes, in_specs=[hbm] * 10, out_specs=(hb...  51.9 us
    pallas_call x1, Pallas kernels, on_device(): pl.pallas_call(store, out_shape=shapes, in_specs=[hbm] * 8, out_specs=(hb...  2.05 us

profile of v5, /device:TPU:1, one launch (start us, length us, event | category | flops | bytes accessed | tf_op | source)
XLA Modules:
  0.0 54.6 jit_solution(5711936950235972803)
XLA Ops:
  0.6 51.9 %shard_map.161 = (bf16[256,256]{1,0:T(8,128)(2,1)}, bf16[256,256]{1,0:T(8,128)(2,1)}, bf16[256,256]{1,0:T(8,128)(2,1)}, bf16[256,256]{1,0:T(8,128)(2,1)}, bf16[2...) custom-call(bf16[256,256]{1,0:T(8,128)(2,1)} %refs_0_.1, ...), custom_call_target="tpu_custom_call" | custom-call | tf_op jit(solution)/shard_map/pallas_call | solution.py:824
  52.5 2.1 %shard_map.162 = (bf16[256,256]{1,0:T(8,128)(2,1)}, bf16[256,256]{1,0:T(8,128)(2,1)}, bf16[256,256]{1,0:T(8,128)(2,1)}, bf16[256,256]{1,0:T(8,128)(2,1)}, bf16[2...) custom-call(bf16[256,256]{1,0:T(8,128)(2,1)} %get-tuple-element.24.refs_0_, ...), custom_call_target="tpu_custom_call" | custom-call | tf_op jit(solution)/shard_map/pallas_call | solution.py:834
